TPU v7x, 256 devices: a whole 4x4x8 slice. The times are simulated.
256 devices in a mesh: ctx: 32 (over z, y_lo, core), head: 8 (over x, y_hi).
Axes of the slice: x: 4, y: 4 (y_hi: 2, y_lo: 2; y = y_hi * 2 + y_lo), z: 8, core: 2. Of those that a mesh axis runs over, the one named last changes fastest.
Arguments:
- queries: bfloat16 [8192, 8192], P(('ctx', 'head')), may hold values from -8 to 8
- keys: bfloat16 [8192, 1024], P(('ctx', 'head')), may hold values from -8 to 8
- values: bfloat16 [8192, 1024], P(('ctx', 'head')), may hold values from -3 to 3
- out_grad: bfloat16 [8192, 8192], P(('ctx', 'head')), may hold values from -3 to 3
- doc_ids: int32 [8192], replicated, may hold values from 0 to 31, never falling along the last dimension, each value on 1 to 4096 neighbouring positions
- block_order: int32 [64], replicated, may hold values from 0 to 63, each once
Outputs:
- attended: bfloat16 [8192, 8192], P(('ctx', 'head'))
- query_grad: bfloat16 [8192, 8192], P(('ctx', 'head'))
- key_grad: bfloat16 [8192, 1024], P(('ctx', 'head'))
- value_grad: bfloat16 [8192, 1024], P(('ctx', 'head'))
Inputs may be any that keep to these rules, and one draw needn't show every extreme that they name: `doc_ids`: documents are numbered in packed order, each one contiguous. `block_order`: each block once.
All inputs are finite; a program needn't handle non-finite values.
Results may differ from a plain program's by a relative error of at most 0.038.
Values may be sent and summed in bfloat16 or wider, within the bound.
A program may use at most 64 MiB of HBM per device.

v0:
```python
import math

import jax
import jax.numpy as jnp
from jax import lax
from jax.sharding import PartitionSpec as P

QH = 64
KVH = 8
HD = 128
BLK = 128


def passed_along(shard, axis, by):
    devices = lax.axis_size(axis)
    return lax.ppermute(shard, axis, [(i, (i + by) % devices) for i in range(devices)])


def token_meta(start, count, block_order, doc_ids):
    index = start + jnp.arange(count, dtype=jnp.int32)
    place = jnp.take(block_order, index // BLK) * BLK + index % BLK
    return (place, jnp.take(doc_ids, place))


def per_device(queries, keys, values, out_grad, doc_ids, block_order):
    ranks = lax.axis_size("ctx")
    rank = lax.axis_index("ctx")
    q_loc, k_loc, v_loc, g_loc = (
        lax.all_to_all(queries, "head", split_axis=1, concat_axis=0, tiled=True),
        lax.all_to_all(keys, "head", split_axis=1, concat_axis=0, tiled=True),
        lax.all_to_all(values, "head", split_axis=1, concat_axis=0, tiled=True),
        lax.all_to_all(out_grad, "head", split_axis=1, concat_axis=0, tiled=True),
    )
    rows = q_loc.shape[0]
    groups = k_loc.shape[1] // HD
    repeat = QH // KVH
    scale = 1.0 / math.sqrt(HD)
    q_grp = q_loc.reshape(rows, groups, repeat, HD)
    g_grp = g_loc.reshape(rows, groups, repeat, HD)
    k_grp = k_loc.reshape(rows, groups, HD)
    v_grp = v_loc.reshape(rows, groups, HD)
    q_place, q_doc = token_meta(rank * rows, rows, block_order, doc_ids)

    def visible_for(key_start, count):
        k_place, k_doc = token_meta(key_start, count, block_order, doc_ids)
        return (q_doc[:, None] == k_doc[None, :]) & (k_place[None, :] <= q_place[:, None])

    def scores(key_rows, visible):
        score = (
            jnp.einsum("qgrd,kgd->grqk", q_grp, key_rows, preferred_element_type=jnp.float32)
            * scale
        )
        return jnp.where(visible[None, None], score, -jnp.inf)

    def forward_tile(state, key_rows, value_rows, key_start):
        visible = visible_for(key_start, key_rows.shape[0])

        def forward_work(current):
            run_max, run_sum, acc = current
            score = scores(key_rows, visible)
            new_max = jnp.maximum(run_max, jnp.max(score, axis=-1))
            prob = jnp.exp(score - new_max[..., None])
            factor = jnp.exp(run_max - new_max)
            run_sum = factor * run_sum + jnp.sum(prob, axis=-1)
            part = jnp.einsum(
                "grqk,kgd->grqd",
                prob.astype(jnp.bfloat16),
                value_rows,
                preferred_element_type=jnp.float32,
            )
            return (new_max, run_sum, factor[..., None] * acc + part)

        return lax.cond(jnp.any(visible), forward_work, lambda current: current, state)

    start_state = (
        jnp.full((groups, repeat, rows), -1e30, jnp.float32),
        jnp.zeros((groups, repeat, rows), jnp.float32),
        jnp.zeros((groups, repeat, rows, HD), jnp.float32),
    )

    def score_grads(key_rows, value_rows, visible, lse, delta):
        score = scores(key_rows, visible)
        prob = jnp.exp(score - lse[..., None]).astype(jnp.bfloat16)
        dprob = jnp.einsum("qgrd,kgd->grqk", g_grp, value_rows, preferred_element_type=jnp.float32)
        dscore = (prob.astype(jnp.float32) * (dprob - delta[..., None])).astype(jnp.bfloat16)
        return (prob, dscore)

    def key_terms(prob, dscore):
        dk_part = jnp.einsum("grqk,qgrd->kgd", dscore, q_grp, preferred_element_type=jnp.float32)
        dv_part = jnp.einsum("grqk,qgrd->kgd", prob, g_grp, preferred_element_type=jnp.float32)
        return (dk_part, dv_part)

    def query_term(dscore, key_rows):
        return jnp.einsum("grqk,kgd->qgrd", dscore, key_rows, preferred_element_type=jnp.float32)

    state = forward_tile(start_state, k_grp, v_grp, rank * rows)

    def forward_step(step, carry):
        key_rows, value_rows, current = carry
        key_rows, value_rows = passed_along((key_rows, value_rows), "ctx", 1)
        source = (rank - step) % ranks
        return (key_rows, value_rows, forward_tile(current, key_rows, value_rows, source * rows))

    unused_k, unused_v, state = lax.fori_loop(1, ranks, forward_step, (k_grp, v_grp, state))
    run_max, run_sum, acc = state
    lse = run_max + jnp.log(run_sum)
    attended = (acc / run_sum[..., None]).astype(jnp.bfloat16)
    delta = jnp.einsum("qgrd,grqd->grq", g_grp, attended, preferred_element_type=jnp.float32)
    zero_query = jnp.zeros((rows, groups, repeat, HD), jnp.float32)
    zero_keys = jnp.zeros((rows, groups, HD), jnp.float32)

    def backward_tile(query_sum, key_rows, value_rows, key_start):
        visible = visible_for(key_start, key_rows.shape[0])

        def backward_work(current):
            prob, dscore = score_grads(key_rows, value_rows, visible, lse, delta)
            dk_part, dv_part = key_terms(prob, dscore)
            return (current + query_term(dscore, key_rows), dk_part, dv_part)

        def skip(current):
            return (current, zero_keys, zero_keys)

        return lax.cond(jnp.any(visible), backward_work, skip, query_sum)

    query_sum, dk_acc, dv_acc = backward_tile(zero_query, k_grp, v_grp, rank * rows)

    def backward_step(step, carry):
        key_rows, value_rows, dk_run, dv_run, current = carry
        key_rows, value_rows = passed_along((key_rows, value_rows), "ctx", 1)
        dk_run, dv_run = passed_along((dk_run, dv_run), "ctx", 1)
        source = (rank - step) % ranks
        current, dk_part, dv_part = backward_tile(current, key_rows, value_rows, source * rows)
        return (key_rows, value_rows, dk_run + dk_part, dv_run + dv_part, current)

    unused_k, unused_v, dk_acc, dv_acc, query_sum = lax.fori_loop(
        1, ranks, backward_step, (k_grp, v_grp, dk_acc, dv_acc, query_sum)
    )
    dk_sum, dv_sum = passed_along((dk_acc, dv_acc), "ctx", 1)
    out_rows = attended.transpose(2, 0, 1, 3).reshape(rows, groups * repeat * HD)
    query_grad = (query_sum * scale).astype(jnp.bfloat16).reshape(rows, groups * repeat * HD)
    key_grad = (dk_sum * scale).astype(jnp.bfloat16).reshape(rows, groups * HD)
    value_grad = dv_sum.astype(jnp.bfloat16).reshape(rows, groups * HD)
    return (
        lax.all_to_all(out_rows, "head", split_axis=0, concat_axis=1, tiled=True),
        lax.all_to_all(query_grad, "head", split_axis=0, concat_axis=1, tiled=True),
        lax.all_to_all(key_grad, "head", split_axis=0, concat_axis=1, tiled=True),
        lax.all_to_all(value_grad, "head", split_axis=0, concat_axis=1, tiled=True),
    )


def solution(mesh):
    return jax.shard_map(
        per_device,
        mesh=mesh,
        in_specs=(
            P(("ctx", "head"), None),
            P(("ctx", "head"), None),
            P(("ctx", "head"), None),
            P(("ctx", "head"), None),
            P(),
            P(),
        ),
        out_specs=(
            P(("ctx", "head"), None),
            P(("ctx", "head"), None),
            P(("ctx", "head"), None),
            P(("ctx", "head"), None),
        ),
        check_vma=False,
    )
```

profile of v0, /device:TPU:1, one launch (start us, length us, event | category | flops | bytes accessed | tf_op | source)
XLA Modules:
  0.0 694.5 jit_solution(17575079252467372248)
XLA Ops:
  2.1 7.5 %all-to-all-start = ((bf16[32,8,128]{2,0,1:T(8,128)(2,1)}), bf16[32,8,128]{2,0,1:T(8,128)(2,1)S(1)}, u32[]{:S(2)}, u32[]{:S(2)}) async-start(bf16[32,8,128]{2,0,1:T(8,128)(2,1)} %copy_bitcast_fusion.5), calls=%async_computation | async-start | bytes 131072 | tf_op jit(solution)/shard_map/all_to_all | solution.py:30
  11.1 5.1 all-to-all-done
  16.2 3.4 all-to-all-start.1
  21.5 4.7 all-to-all-done.1
  26.1 3.6 all-to-all-start.2
  32.5 5.7 all-to-all-done.2
  38.3 3.5 all-to-all-start.4
  45.2 5.0 all-to-all-done.4
  51.9 247.9 %while.51 = (s32[]{:T(128)}, bf16[256,1,128]{2,0,1:T(8,128)(2,1)S(1)}, bf16[256,1,128]{2,0,1:T(8,128)(2,1)S(1)}, f32[1,8,256]{2,1,0:T(8,128)S(1)}, f32[1,8,256]{...) while((s32[]{:T(128)}, ...), condition=%wide.region_11.14_spmd, body=%wide.region_5.13_spmd.sunk | while | flops 272914944 | bytes 10120688 | solution.py:104
  52.0 5.8 collective-permute-start
  63.1 4.4 collective-permute-start
  95.8 3.3 collective-permute-start.1
  262.7 3.7 collective-permute-start.1
  305.1 339.1 %while.52 = (s32[]{:T(128)}, bf16[256,1,128]{2,0,1:T(8,128)(2,1)S(1)}, bf16[256,1,128]{2,0,1:T(8,128)(2,1)S(1)}, f32[256,1,128]{2,0,1:T(8,128)}, f32[256,1,128]{...) while((s32[]{:T(128)}, ...), condition=%wide.region_18.21_spmd, body=%wide.region_14.20_spmd.sunk | while | flops 675889664 | bytes 13741632 | solution.py:135
  305.1 4.7 collective-permute-start.2
  316.2 4.3 collective-permute-start.2
  331.3 3.7 collective-permute-start.4
  358.3 5.1 collective-permute-start.2
  382.4 3.1 collective-permute-start.4
  426.7 4.6 collective-permute-start.5
  458.5 3.2 collective-permute-start.2
  479.3 3.1 collective-permute-start.4
  533.2 5.1 collective-permute-start.4
  632.1 6.3 collective-permute-start.4
  649.7 3.6 all-to-all-start.7
  653.9 6.0 all-to-all-done.7
  659.9 3.4 all-to-all-start.6
  664.7 5.0 all-to-all-done.6
  669.8 3.5 all-to-all-start.5
  674.6 7.1 %all-to-all-done.5 = bf16[8,32,1024]{2,1,0:T(8,128)(2,1)S(1)} async-done(((bf16[8,32,1024]{2,1,0:T(8,128)(2,1)}), bf16[8,32,1024]{2,1,0:T(8,128)(2,1)S(1)}, u32[]{:S(2)}, u32[]{:S(2)}) %all-to-all-start.5) | async-done | bytes 524320 | tf_op jit(solution)/shard_map/all_to_all | solution.py:145
  681.7 3.5 all-to-all-start.3
  687.3 6.3 all-to-all-done.3
  (1432 shorter events, 608.1 us)
Async XLA Ops:
  2.1 14.1 %all-to-all-start = ((bf16[32,8,128]{2,0,1:T(8,128)(2,1)}), bf16[32,8,128]{2,0,1:T(8,128)(2,1)S(1)}, u32[]{:S(2)}, u32[]{:S(2)}) async-start(bf16[32,8,128]{2,0,1:T(8,128)(2,1)} %copy_bitcast_fusion.5), calls=%async_computation | async-start | bytes 131072 | tf_op jit(solution)/shard_map/all_to_all | solution.py:30
  26.1 12.2 %all-to-all-start.2 = ((bf16[32,8,1024]{2,0,1:T(8,128)(2,1)}), bf16[32,8,1024]{2,0,1:T(8,128)(2,1)S(1)}, u32[]{:S(2)}, u32[]{:S(2)}) async-start(bf16[32,8,1024]{2,0,1:T(8,128)(2,1)} %bitcast.281), calls=%async_computation.2 | async-start | bytes 1048576 | tf_op jit(solution)/shard_map/all_to_all | solution.py:29
  38.3 11.9 %all-to-all-start.4 = ((bf16[32,8,1024]{2,0,1:T(8,128)(2,1)}), bf16[32,8,1024]{2,0,1:T(8,128)(2,1)S(1)}, u32[]{:S(2)}, u32[]{:S(2)}) async-start(bf16[32,8,1024]{2,0,1:T(8,128)(2,1)} %bitcast.280), calls=%async_computation.4 | async-start | bytes 1048576 | tf_op jit(solution)/shard_map/all_to_all | solution.py:32
  52.0 11.0 %collective-permute-start = (bf16[256,1,128]{2,0,1:T(8,128)(2,1)S(1)}, bf16[256,1,128]{2,0,1:T(8,128)(2,1)S(1)}, u32[]{:S(2)}, u32[]{:S(2)}) collective-permute-start(bf16[256,1,128]{2,0,1:T(8,128)(2,1)S(1)} %get-tuple-element.1329), channel_id=1, source_target_pairs={{0,8},{8,16},{16,24},{24,32},{32,40},{40,48},{48,56},{56,64},{64,7... | collective-permute-start | bytes 196616 | tf_op jit(solution)/shard_map/while/body/eval_jaxpr/ppermute | solution.py:16
  94.0 10.3 %collective-permute-start = (bf16[256,1,128]{2,0,1:T(8,128)(2,1)S(1)}, bf16[256,1,128]{2,0,1:T(8,128)(2,1)S(1)}, u32[]{:S(2)}, u32[]{:S(2)}) collective-permute-start(bf16[256,1,128]{2,0,1:T(8,128)(2,1)S(1)} %get-tuple-element.1329), channel_id=1, source_target_pairs={{0,8},{8,16},{16,24},{24,32},{32,40},{40,48},{48,56},{56,64},{64,7... | collective-permute-start | bytes 196616 | tf_op jit(solution)/shard_map/while/body/eval_jaxpr/ppermute | solution.py:16
  260.9 10.5 %collective-permute-start = (bf16[256,1,128]{2,0,1:T(8,128)(2,1)S(1)}, bf16[256,1,128]{2,0,1:T(8,128)(2,1)S(1)}, u32[]{:S(2)}, u32[]{:S(2)}) collective-permute-start(bf16[256,1,128]{2,0,1:T(8,128)(2,1)S(1)} %get-tuple-element.1329), channel_id=1, source_target_pairs={{0,8},{8,16},{16,24},{24,32},{32,40},{40,48},{48,56},{56,64},{64,7... | collective-permute-start | bytes 196616 | tf_op jit(solution)/shard_map/while/body/eval_jaxpr/ppermute | solution.py:16
  305.1 10.2 %collective-permute-start.2 = (bf16[256,1,128]{2,0,1:T(8,128)(2,1)S(1)}, bf16[256,1,128]{2,0,1:T(8,128)(2,1)S(1)}, u32[]{:S(2)}, u32[]{:S(2)}) collective-permute-start(bf16[256,1,128]{2,0,1:T(8,128)(2,1)S(1)} %get-tuple-element.1389), channel_id=1, source_target_pairs={{0,8},{8,16},{16,24},{24,32},{32,40},{40,48},{48,56},{56,64},{64,7... | collective-permute-start | bytes 196616 | tf_op jit(solution)/shard_map/while/body/eval_jaxpr/ppermute | solution.py:16
  316.2 11.4 %collective-permute-start.2 = (bf16[256,1,128]{2,0,1:T(8,128)(2,1)S(1)}, bf16[256,1,128]{2,0,1:T(8,128)(2,1)S(1)}, u32[]{:S(2)}, u32[]{:S(2)}) collective-permute-start(bf16[256,1,128]{2,0,1:T(8,128)(2,1)S(1)} %get-tuple-element.1389), channel_id=1, source_target_pairs={{0,8},{8,16},{16,24},{24,32},{32,40},{40,48},{48,56},{56,64},{64,7... | collective-permute-start | bytes 196616 | tf_op jit(solution)/shard_map/while/body/eval_jaxpr/ppermute | solution.py:16
  331.1 11.7 %collective-permute-start.5 = (f32[256,1,128]{2,0,1:T(8,128)S(1)}, f32[256,1,128]{2,0,1:T(8,128)S(1)}, u32[]{:S(2)}, u32[]{:S(2)}) collective-permute-start(f32[256,1,128]{2,0,1:T(8,128)S(1)} %get-tuple-element.1392), channel_id=1, source_target_pairs={{0,8},{8,16},{16,24},{24,32},{32,40},{40,48},{48,56},{56,64},{64,7... | collective-permute-start | bytes 393224 | tf_op jit(solution)/shard_map/while/body/eval_jaxpr/ppermute | solution.py:16
  331.3 11.5 %collective-permute-start.4 = (f32[256,1,128]{2,0,1:T(8,128)}, f32[256,1,128]{2,0,1:T(8,128)S(1)}, u32[]{:S(2)}, u32[]{:S(2)}) collective-permute-start(f32[256,1,128]{2,0,1:T(8,128)} %get-tuple-element.1391), channel_id=1, source_target_pairs={{0,8},{8,16},{16,24},{24,32},{32,40},{40,48},{48,56},{56,64},{64,7... | collective-permute-start | bytes 393224 | tf_op jit(solution)/shard_map/while/body/eval_jaxpr/ppermute | solution.py:16
  358.3 11.7 %collective-permute-start.2 = (bf16[256,1,128]{2,0,1:T(8,128)(2,1)S(1)}, bf16[256,1,128]{2,0,1:T(8,128)(2,1)S(1)}, u32[]{:S(2)}, u32[]{:S(2)}) collective-permute-start(bf16[256,1,128]{2,0,1:T(8,128)(2,1)S(1)} %get-tuple-element.1389), channel_id=1, source_target_pairs={{0,8},{8,16},{16,24},{24,32},{32,40},{40,48},{48,56},{56,64},{64,7... | collective-permute-start | bytes 196616 | tf_op jit(solution)/shard_map/while/body/eval_jaxpr/ppermute | solution.py:16
  382.2 11.1 %collective-permute-start.5 = (f32[256,1,128]{2,0,1:T(8,128)S(1)}, f32[256,1,128]{2,0,1:T(8,128)S(1)}, u32[]{:S(2)}, u32[]{:S(2)}) collective-permute-start(f32[256,1,128]{2,0,1:T(8,128)S(1)} %get-tuple-element.1392), channel_id=1, source_target_pairs={{0,8},{8,16},{16,24},{24,32},{32,40},{40,48},{48,56},{56,64},{64,7... | collective-permute-start | bytes 393224 | tf_op jit(solution)/shard_map/while/body/eval_jaxpr/ppermute | solution.py:16
  382.4 10.9 %collective-permute-start.4 = (f32[256,1,128]{2,0,1:T(8,128)}, f32[256,1,128]{2,0,1:T(8,128)S(1)}, u32[]{:S(2)}, u32[]{:S(2)}) collective-permute-start(f32[256,1,128]{2,0,1:T(8,128)} %get-tuple-element.1391), channel_id=1, source_target_pairs={{0,8},{8,16},{16,24},{24,32},{32,40},{40,48},{48,56},{56,64},{64,7... | collective-permute-start | bytes 393224 | tf_op jit(solution)/shard_map/while/body/eval_jaxpr/ppermute | solution.py:16
  424.1 12.3 %collective-permute-start.2 = (bf16[256,1,128]{2,0,1:T(8,128)(2,1)S(1)}, bf16[256,1,128]{2,0,1:T(8,128)(2,1)S(1)}, u32[]{:S(2)}, u32[]{:S(2)}) collective-permute-start(bf16[256,1,128]{2,0,1:T(8,128)(2,1)S(1)} %get-tuple-element.1389), channel_id=1, source_target_pairs={{0,8},{8,16},{16,24},{24,32},{32,40},{40,48},{48,56},{56,64},{64,7... | collective-permute-start | bytes 196616 | tf_op jit(solution)/shard_map/while/body/eval_jaxpr/ppermute | solution.py:16
  424.1 12.3 %collective-permute-start.3 = (bf16[256,1,128]{2,0,1:T(8,128)(2,1)S(1)}, bf16[256,1,128]{2,0,1:T(8,128)(2,1)S(1)}, u32[]{:S(2)}, u32[]{:S(2)}) collective-permute-start(bf16[256,1,128]{2,0,1:T(8,128)(2,1)S(1)} %get-tuple-element.1390), channel_id=1, source_target_pairs={{0,8},{8,16},{16,24},{24,32},{32,40},{40,48},{48,56},{56,64},{64,7... | collective-permute-start | bytes 196616 | tf_op jit(solution)/shard_map/while/body/eval_jaxpr/ppermute | solution.py:16
  426.7 12.4 %collective-permute-start.5 = (f32[256,1,128]{2,0,1:T(8,128)S(1)}, f32[256,1,128]{2,0,1:T(8,128)S(1)}, u32[]{:S(2)}, u32[]{:S(2)}) collective-permute-start(f32[256,1,128]{2,0,1:T(8,128)S(1)} %get-tuple-element.1392), channel_id=1, source_target_pairs={{0,8},{8,16},{16,24},{24,32},{32,40},{40,48},{48,56},{56,64},{64,7... | collective-permute-start | bytes 393224 | tf_op jit(solution)/shard_map/while/body/eval_jaxpr/ppermute | solution.py:16
  479.1 11.1 %collective-permute-start.5 = (f32[256,1,128]{2,0,1:T(8,128)S(1)}, f32[256,1,128]{2,0,1:T(8,128)S(1)}, u32[]{:S(2)}, u32[]{:S(2)}) collective-permute-start(f32[256,1,128]{2,0,1:T(8,128)S(1)} %get-tuple-element.1392), channel_id=1, source_target_pairs={{0,8},{8,16},{16,24},{24,32},{32,40},{40,48},{48,56},{56,64},{64,7... | collective-permute-start | bytes 393224 | tf_op jit(solution)/shard_map/while/body/eval_jaxpr/ppermute | solution.py:16
  479.3 11.0 %collective-permute-start.4 = (f32[256,1,128]{2,0,1:T(8,128)}, f32[256,1,128]{2,0,1:T(8,128)S(1)}, u32[]{:S(2)}, u32[]{:S(2)}) collective-permute-start(f32[256,1,128]{2,0,1:T(8,128)} %get-tuple-element.1391), channel_id=1, source_target_pairs={{0,8},{8,16},{16,24},{24,32},{32,40},{40,48},{48,56},{56,64},{64,7... | collective-permute-start | bytes 393224 | tf_op jit(solution)/shard_map/while/body/eval_jaxpr/ppermute | solution.py:16
  511.2 11.1 %collective-permute-start.5 = (f32[256,1,128]{2,0,1:T(8,128)S(1)}, f32[256,1,128]{2,0,1:T(8,128)S(1)}, u32[]{:S(2)}, u32[]{:S(2)}) collective-permute-start(f32[256,1,128]{2,0,1:T(8,128)S(1)} %get-tuple-element.1392), channel_id=1, source_target_pairs={{0,8},{8,16},{16,24},{24,32},{32,40},{40,48},{48,56},{56,64},{64,7... | collective-permute-start | bytes 393224 | tf_op jit(solution)/shard_map/while/body/eval_jaxpr/ppermute | solution.py:16
  533.1 10.3 %collective-permute-start.2 = (bf16[256,1,128]{2,0,1:T(8,128)(2,1)S(1)}, bf16[256,1,128]{2,0,1:T(8,128)(2,1)S(1)}, u32[]{:S(2)}, u32[]{:S(2)}) collective-permute-start(bf16[256,1,128]{2,0,1:T(8,128)(2,1)S(1)} %get-tuple-element.1389), channel_id=1, source_target_pairs={{0,8},{8,16},{16,24},{24,32},{32,40},{40,48},{48,56},{56,64},{64,7... | collective-permute-start | bytes 196616 | tf_op jit(solution)/shard_map/while/body/eval_jaxpr/ppermute | solution.py:16
  533.2 10.3 %collective-permute-start.3 = (bf16[256,1,128]{2,0,1:T(8,128)(2,1)S(1)}, bf16[256,1,128]{2,0,1:T(8,128)(2,1)S(1)}, u32[]{:S(2)}, u32[]{:S(2)}) collective-permute-start(bf16[256,1,128]{2,0,1:T(8,128)(2,1)S(1)} %get-tuple-element.1390), channel_id=1, source_target_pairs={{0,8},{8,16},{16,24},{24,32},{32,40},{40,48},{48,56},{56,64},{64,7... | collective-permute-start | bytes 196616 | tf_op jit(solution)/shard_map/while/body/eval_jaxpr/ppermute | solution.py:16
  533.2 12.9 %collective-permute-start.5 = (f32[256,1,128]{2,0,1:T(8,128)S(1)}, f32[256,1,128]{2,0,1:T(8,128)S(1)}, u32[]{:S(2)}, u32[]{:S(2)}) collective-permute-start(f32[256,1,128]{2,0,1:T(8,128)S(1)} %get-tuple-element.1392), channel_id=1, source_target_pairs={{0,8},{8,16},{16,24},{24,32},{32,40},{40,48},{48,56},{56,64},{64,7... | collective-permute-start | bytes 393224 | tf_op jit(solution)/shard_map/while/body/eval_jaxpr/ppermute | solution.py:16
  533.2 12.9 %collective-permute-start.4 = (f32[256,1,128]{2,0,1:T(8,128)}, f32[256,1,128]{2,0,1:T(8,128)S(1)}, u32[]{:S(2)}, u32[]{:S(2)}) collective-permute-start(f32[256,1,128]{2,0,1:T(8,128)} %get-tuple-element.1391), channel_id=1, source_target_pairs={{0,8},{8,16},{16,24},{24,32},{32,40},{40,48},{48,56},{56,64},{64,7... | collective-permute-start | bytes 393224 | tf_op jit(solution)/shard_map/while/body/eval_jaxpr/ppermute | solution.py:16
  546.9 11.0 %collective-permute-start.5 = (f32[256,1,128]{2,0,1:T(8,128)S(1)}, f32[256,1,128]{2,0,1:T(8,128)S(1)}, u32[]{:S(2)}, u32[]{:S(2)}) collective-permute-start(f32[256,1,128]{2,0,1:T(8,128)S(1)} %get-tuple-element.1392), channel_id=1, source_target_pairs={{0,8},{8,16},{16,24},{24,32},{32,40},{40,48},{48,56},{56,64},{64,7... | collective-permute-start | bytes 393224 | tf_op jit(solution)/shard_map/while/body/eval_jaxpr/ppermute | solution.py:16
  605.8 10.8 %collective-permute-start.2 = (bf16[256,1,128]{2,0,1:T(8,128)(2,1)S(1)}, bf16[256,1,128]{2,0,1:T(8,128)(2,1)S(1)}, u32[]{:S(2)}, u32[]{:S(2)}) collective-permute-start(bf16[256,1,128]{2,0,1:T(8,128)(2,1)S(1)} %get-tuple-element.1389), channel_id=1, source_target_pairs={{0,8},{8,16},{16,24},{24,32},{32,40},{40,48},{48,56},{56,64},{64,7... | collective-permute-start | bytes 196616 | tf_op jit(solution)/shard_map/while/body/eval_jaxpr/ppermute | solution.py:16
  617.5 11.7 %collective-permute-start.5 = (f32[256,1,128]{2,0,1:T(8,128)S(1)}, f32[256,1,128]{2,0,1:T(8,128)S(1)}, u32[]{:S(2)}, u32[]{:S(2)}) collective-permute-start(f32[256,1,128]{2,0,1:T(8,128)S(1)} %get-tuple-element.1392), channel_id=1, source_target_pairs={{0,8},{8,16},{16,24},{24,32},{32,40},{40,48},{48,56},{56,64},{64,7... | collective-permute-start | bytes 393224 | tf_op jit(solution)/shard_map/while/body/eval_jaxpr/ppermute | solution.py:16
  629.9 13.5 %collective-permute-start.2 = (bf16[256,1,128]{2,0,1:T(8,128)(2,1)S(1)}, bf16[256,1,128]{2,0,1:T(8,128)(2,1)S(1)}, u32[]{:S(2)}, u32[]{:S(2)}) collective-permute-start(bf16[256,1,128]{2,0,1:T(8,128)(2,1)S(1)} %get-tuple-element.1389), channel_id=1, source_target_pairs={{0,8},{8,16},{16,24},{24,32},{32,40},{40,48},{48,56},{56,64},{64,7... | collective-permute-start | bytes 196616 | tf_op jit(solution)/shard_map/while/body/eval_jaxpr/ppermute | solution.py:16
  629.9 13.5 %collective-permute-start.3 = (bf16[256,1,128]{2,0,1:T(8,128)(2,1)S(1)}, bf16[256,1,128]{2,0,1:T(8,128)(2,1)S(1)}, u32[]{:S(2)}, u32[]{:S(2)}) collective-permute-start(bf16[256,1,128]{2,0,1:T(8,128)(2,1)S(1)} %get-tuple-element.1390), channel_id=1, source_target_pairs={{0,8},{8,16},{16,24},{24,32},{32,40},{40,48},{48,56},{56,64},{64,7... | collective-permute-start | bytes 196616 | tf_op jit(solution)/shard_map/while/body/eval_jaxpr/ppermute | solution.py:16
  629.9 13.6 %collective-permute-start.5 = (f32[256,1,128]{2,0,1:T(8,128)S(1)}, f32[256,1,128]{2,0,1:T(8,128)S(1)}, u32[]{:S(2)}, u32[]{:S(2)}) collective-permute-start(f32[256,1,128]{2,0,1:T(8,128)S(1)} %get-tuple-element.1392), channel_id=1, source_target_pairs={{0,8},{8,16},{16,24},{24,32},{32,40},{40,48},{48,56},{56,64},{64,7... | collective-permute-start | bytes 393224 | tf_op jit(solution)/shard_map/while/body/eval_jaxpr/ppermute | solution.py:16
  632.1 11.5 %collective-permute-start.4 = (f32[256,1,128]{2,0,1:T(8,128)}, f32[256,1,128]{2,0,1:T(8,128)S(1)}, u32[]{:S(2)}, u32[]{:S(2)}) collective-permute-start(f32[256,1,128]{2,0,1:T(8,128)} %get-tuple-element.1391), channel_id=1, source_target_pairs={{0,8},{8,16},{16,24},{24,32},{32,40},{40,48},{48,56},{56,64},{64,7... | collective-permute-start | bytes 393224 | tf_op jit(solution)/shard_map/while/body/eval_jaxpr/ppermute | solution.py:16
  669.8 12.0 %all-to-all-start.5 = ((bf16[8,32,1024]{2,1,0:T(8,128)(2,1)}), bf16[8,32,1024]{2,1,0:T(8,128)(2,1)S(1)}, u32[]{:S(2)}, u32[]{:S(2)}) async-start(bf16[8,32,1024]{2,1,0:T(8,128)(2,1)} %all_to_all.120), calls=%async_computation.5 | async-start | bytes 1048576 | tf_op jit(solution)/shard_map/all_to_all | solution.py:145
  681.7 11.9 %all-to-all-start.3 = ((bf16[8,32,1024]{2,1,0:T(8,128)(2,1)}), bf16[8,32,1024]{2,1,0:T(8,128)(2,1)S(1)}, u32[]{:S(2)}, u32[]{:S(2)}) async-start(bf16[8,32,1024]{2,1,0:T(8,128)(2,1)} %all_to_all.113), calls=%async_computation.3 | async-start | bytes 1048576 | tf_op jit(solution)/shard_map/all_to_all | solution.py:144
  (170 other events, 1208.1 us)
where the time goes:
time: 699 us; the launch traced here: 695 us
  local copies, waits for them, and re-layouts  240 us (34%)
  starting transfers between devices  180 us (26%)
  matrix products  91.5 us (13%)
  other arithmetic  83.5 us (12%)
  loops' own time  50.1 us (7%)
  waiting for transfers between devices  48.2 us (7%)
    ppermute x188, starting transfers between devices, passed_along(): lax.ppermute(shard, axis, [(i, (i + by) % devices) for i in range(devices)])  148 us
    gather x63, local copies, waits for them, and re-layouts, token_meta(): place = jnp.take(block_order, index // BLK) * BLK + index % BLK  118 us
    gather x63, local copies, waits for them, and re-layouts, token_meta(): return (place, jnp.take(doc_ids, place))  108 us
    dot_general x48, matrix products, scores(): jnp.einsum('qgrd,kgd->grqk', q_grp, key_rows, preferred_element_type=jnp....  25.5 us
    reduce_or x31, other arithmetic, forward_tile(): jnp.any(visible)  23.9 us
    reduce_or x31, other arithmetic, backward_tile(): return lax.cond(jnp.any(visible), backward_work, skip, query_sum)  23.9 us
    another operation x1, loops' own time, per_device(): lax.fori_loop(1, ranks, backward_step, (k_grp, v_grp, dk_acc, dv_acc, que...  23.5 us
    another operation x1, loops' own time, per_device(): lax.fori_loop(1, ranks, forward_step, (k_grp, v_grp, state))  23.3 us
  transfers between devices with their start and end apart: 196, of which 9 were waited for; matrix products, arithmetic and copies ran while one was open for 50% of the time, Pallas kernels for 0%

commit v1 on v0

v1 whole, which is shorter than its diff:
```python
import functools
import math

import jax
import jax.numpy as jnp
from jax import lax
from jax.experimental import pallas as pl
from jax.experimental.pallas import tpu as pltpu
from jax.sharding import PartitionSpec as P

QH = 64
KVH = 8
HD = 128
BLK = 128
NS = 4
KTILE = 512
LOG2E = math.log2(math.e)
SCALE = 1.0 / math.sqrt(HD)
NEG = -1e30
MESH = pl.DeviceIdType.MESH
F32 = jnp.float32
BF16 = jnp.bfloat16
NT = (((1,), (1,)), ((), ()))
NN = (((1,), (0,)), ((), ()))
VMEM_LIMIT = 56 * 1024 * 1024


def dot(a, b, dims):
    return lax.dot_general(a, b, dims, preferred_element_type=F32)


class Where:
    def __init__(self, planes, groups):
        ctx = lax.axis_index("ctx")
        self.planes, self.groups = planes, groups
        self.size = NS * groups
        self.g = lax.axis_index("head")
        self.z, self.s = ctx // NS, ctx % NS
        self.core, self.ylo = self.s % 2, self.s // 2
        self.p = self.s * groups + self.g
        self.up = (((self.z + 1) % planes) * NS + self.s, self.g)
        self.down = (((self.z + planes - 1) % planes) * NS + self.s, self.g)
        self.sib = (ctx + 1 - 2 * self.core, self.g)

    def peer(self, i):
        o = (self.p + i) % self.size
        return o, o // self.groups, o % self.groups, (self.z * NS + o // self.groups, o % self.groups)

    def greet(self):
        bar = pltpu.get_barrier_semaphore()

        def signal(i, carry):
            pl.semaphore_signal(bar, inc=1, device_id=self.peer(i)[3], device_id_type=MESH)
            return carry

        lax.fori_loop(1, self.size, signal, 0)
        for other in (self.up, self.down):
            pl.semaphore_signal(bar, inc=1, device_id=other, device_id_type=MESH)
        pl.semaphore_wait(bar, self.size + 1)


def remote(src, dst, send, recv, device):
    return pltpu.make_async_remote_copy(
        src_ref=src, dst_ref=dst, send_sem=send, recv_sem=recv, device_id=device, device_id_type=MESH
    )


def aligned(index, size):
    return pl.ds(pl.multiple_of(index * size, size), size)


def gather_kernel(planes, groups, q_ref, k_ref, v_ref, g_ref, qo_ref, go_ref, kv_ref,
                  local, a2a_send, a2a_recv, z_send, z_recv, sib_send, sib_recv):
    at = Where(planes, groups)
    rows = q_ref.shape[0]
    wide = q_ref.shape[1] // (NS * groups)
    half_rows = kv_ref.shape[2] // 2
    mine = aligned(at.p, rows)
    cols_own = aligned(at.g, HD)

    own_q = pltpu.make_async_copy(q_ref.at[:, aligned(at.g * NS + at.s, wide)], qo_ref.at[mine], local.at[0])
    own_g = pltpu.make_async_copy(g_ref.at[:, aligned(at.g * NS + at.s, wide)], go_ref.at[mine], local.at[1])
    own_k = pltpu.make_async_copy(k_ref.at[:, cols_own], kv_ref.at[0, at.z, mine], local.at[2])
    own_v = pltpu.make_async_copy(v_ref.at[:, cols_own], kv_ref.at[1, at.z, mine], local.at[2])
    own_q.start()
    own_g.start()

    @pl.when(at.core == 0)
    def _():
        own_k.start()

    @pl.when(at.core == 1)
    def _():
        own_v.start()

    at.greet()

    def send_kv(i, carry):
        _, os, og, device = at.peer(i)
        cols = aligned(og, HD)

        @pl.when(os % 2 == 0)
        def _():
            remote(k_ref.at[:, cols], kv_ref.at[0, at.z, mine], a2a_send.at[0], a2a_recv.at[0], device).start()

        @pl.when(os % 2 == 1)
        def _():
            remote(v_ref.at[:, cols], kv_ref.at[1, at.z, mine], a2a_send.at[0], a2a_recv.at[0], device).start()

        return carry

    lax.fori_loop(1, at.size, send_kv, 0)

    def send_q(i, carry):
        _, os, og, device = at.peer(i)
        cols = aligned(og * NS + os, wide)
        remote(q_ref.at[:, cols], qo_ref.at[mine], a2a_send.at[1], a2a_recv.at[1], device).start()
        remote(g_ref.at[:, cols], go_ref.at[mine], a2a_send.at[2], a2a_recv.at[2], device).start()
        return carry

    lax.fori_loop(1, at.size, send_q, 0)

    others = pl.ds(0, rows * (at.size - 1))
    own_k.wait()
    got = kv_ref.at[at.core, at.z, others]
    remote(got, got, a2a_send.at[0], a2a_recv.at[0], at.up).wait_recv()

    def piece(chunk, half):
        return kv_ref.at[at.core, chunk, pl.ds(half * half_rows, half_rows)]

    own = kv_ref.at[at.core, at.z]
    hops = planes // 2

    def moves(j, half, way):
        return j < hops - 1 or half == way

    def chunk_at(j, way):
        return (at.z + planes - j) % planes if way == 0 else (at.z + j) % planes

    def send(j, half, way):
        ref = piece(chunk_at(j, way), half)
        slot = (way, 2 * j + half)
        return remote(ref, ref, z_send.at[slot], z_recv.at[slot], at.up if way == 0 else at.down)

    def arrival(j, half, way):
        ref = piece(chunk_at(j + 1, way), half)
        slot = (way, 2 * j + half)
        return remote(ref, ref, z_send.at[slot], z_recv.at[slot], at.up if way == 0 else at.down)

    for j in range(hops):
        for half in (0, 1):
            for way in (0, 1):
                if j > 0:
                    arrival(j - 1, half, way).wait_recv()
                if moves(j, half, way):
                    send(j, half, way).start()
                if j > 0:
                    ref = piece(chunk_at(j, way), half)
                    remote(ref, ref, sib_send, sib_recv, at.sib).start()
        if j == 0:
            remote(own, own, sib_send, sib_recv, at.sib).start()
    for way in (0, 1):
        arrival(hops - 1, way, way).wait_recv()
        ref = piece(chunk_at(hops, way), way)
        remote(ref, ref, sib_send, sib_recv, at.sib).start()

    own_q.wait()
    own_g.wait()
    for n, (src, dst) in enumerate(((q_ref, qo_ref), (g_ref, go_ref))):
        sent = src.at[:, pl.ds(0, wide * (at.size - 1))]
        came = dst.at[others]
        remote(came, came, a2a_send.at[n + 1], a2a_recv.at[n + 1], at.up).wait_recv()
        remote(sent, sent, a2a_send.at[n + 1], a2a_recv.at[n + 1], at.up).wait_send()
    remote(got, got, a2a_send.at[0], a2a_recv.at[0], at.up).wait_send()
    for j in range(hops):
        for half in (0, 1):
            for way in (0, 1):
                if moves(j, half, way):
                    send(j, half, way).wait_send()
    sent = kv_ref.at[at.core]
    came = kv_ref.at[1 - at.core]
    remote(sent, sent, sib_send, sib_recv, at.sib).wait_send()
    remote(came, came, sib_send, sib_recv, at.sib).wait_recv()


def gather(planes, groups, queries, keys, values, out_grad):
    rows = queries.shape[0]
    plane_rows = rows * NS * groups
    wide = queries.shape[1] // (NS * groups)
    hops = planes // 2
    any_space = pl.BlockSpec(memory_space=pl.ANY)
    return pl.pallas_call(
        functools.partial(gather_kernel, planes, groups),
        out_shape=(
            jax.ShapeDtypeStruct((plane_rows, wide), BF16),
            jax.ShapeDtypeStruct((plane_rows, wide), BF16),
            jax.ShapeDtypeStruct((2, planes, plane_rows, HD), BF16),
        ),
        in_specs=[any_space] * 4,
        out_specs=(any_space,) * 3,
        scratch_shapes=[
            pltpu.SemaphoreType.DMA((3,)),
            pltpu.SemaphoreType.DMA((3,)),
            pltpu.SemaphoreType.DMA((3,)),
            pltpu.SemaphoreType.DMA((2, 2 * hops)),
            pltpu.SemaphoreType.DMA((2, 2 * hops)),
            pltpu.SemaphoreType.DMA,
            pltpu.SemaphoreType.DMA,
        ],
        compiler_params=pltpu.CompilerParams(collective_id=0, has_side_effects=True),
        name="gather",
    )(queries, keys, values, out_grad)


def attend_kernel(order_ref, doc_ref, plane_ref, q_ref, g_ref, doc2_ref, kv_ref, att_ref, dq_ref, dkv_ref,
                  k_s, v_s, kt_s, vt_s, dk_s, dv_s, s_s, p_s, acc_s, sem):
    tokens = kv_ref.shape[1]
    blocks = tokens // BLK
    own_blocks = q_ref.shape[0] // BLK
    heads = q_ref.shape[1] // HD
    rows = heads * BLK
    padded = k_s.shape[0]

    def fetch(i, carry):
        src, dst = aligned(i, BLK), aligned(order_ref[i], BLK)
        pltpu.make_async_copy(kv_ref.at[0, src], k_s.at[dst], sem.at[0]).start()
        pltpu.make_async_copy(kv_ref.at[1, src], v_s.at[dst], sem.at[1]).start()
        return carry

    lax.fori_loop(0, blocks, fetch, 0)
    tail = pl.ds(tokens, padded - tokens)
    k_s[tail, :] = jnp.zeros((padded - tokens, HD), BF16)
    v_s[tail, :] = jnp.zeros((padded - tokens, HD), BF16)
    kt_s[:, tail] = jnp.zeros((HD, padded - tokens), BF16)
    vt_s[:, tail] = jnp.zeros((HD, padded - tokens), BF16)

    def clear(i, carry):
        at = aligned(i, KTILE)
        dk_s[at, :] = jnp.zeros((KTILE, HD), F32)
        dv_s[at, :] = jnp.zeros((KTILE, HD), F32)
        return carry

    lax.fori_loop(0, padded // KTILE, clear, 0)
    whole = pl.ds(0, tokens)
    pltpu.make_async_copy(kv_ref.at[0], k_s.at[whole], sem.at[0]).wait()
    pltpu.make_async_copy(kv_ref.at[1], v_s.at[whole], sem.at[1]).wait()

    def eye(n):
        return (lax.broadcasted_iota(jnp.int32, (n, n), 0) == lax.broadcasted_iota(jnp.int32, (n, n), 1)).astype(
            F32).astype(BF16)

    eye_d = eye(HD)
    eye_r = eye(rows)

    def turn(i, carry):
        at = aligned(i, KTILE)
        kt_s[:, at] = dot(eye_d, k_s[at, :], NT).astype(BF16)
        vt_s[:, at] = dot(eye_d, v_s[at, :], NT).astype(BF16)
        return carry

    lax.fori_loop(0, tokens // KTILE, turn, 0)

    def query_block(n, carry):
        packed = order_ref[plane_ref[0] * own_blocks + n]
        first = packed * BLK
        doc0 = doc_ref[first]

        def halve(_, span):
            lo, hi = span
            mid = (lo + hi) // 2
            below = doc_ref[mid] < doc0
            return jnp.where(below, mid + 1, lo), jnp.where(below, hi, mid)

        doc_start, _ = lax.fori_loop(0, tokens.bit_length(), halve, (jnp.int32(0), first))
        base = (doc_start // BLK) * BLK
        tiles = (first + BLK - base + KTILE - 1) // KTILE

        lane = lax.broadcasted_iota(jnp.int32, (8, BLK), 1)
        docs = jnp.broadcast_to(doc2_ref[pl.ds(packed, 1), :], (8, BLK))
        opens = (lane > 0) & (docs != pltpu.roll(docs, 1, 1))
        begin = jnp.where(opens, first + lane, doc_start)
        step = 1
        while step < BLK:
            begin = jnp.maximum(begin, jnp.where(lane >= step, pltpu.roll(begin, step, 1), 0))
            step *= 2
        low = jnp.concatenate([begin[:1]] * heads, axis=1) - base
        high = jnp.concatenate([(first + lane)[:1]] * heads, axis=1) - base

        here = aligned(n, BLK)
        qs = jnp.concatenate([q_ref[here, h * HD:(h + 1) * HD] for h in range(heads)], axis=0)
        gs = jnp.concatenate([g_ref[here, h * HD:(h + 1) * HD] for h in range(heads)], axis=0)
        key_at = lax.broadcasted_iota(jnp.int32, (KTILE, rows), 0)

        def score_tile(t, top):
            at = pl.ds(pl.multiple_of(base + t * KTILE, BLK), KTILE)
            score = dot(k_s[at, :], qs, NT) * (SCALE * LOG2E)
            seen = (key_at >= low - t * KTILE) & (key_at <= high - t * KTILE)
            score = jnp.where(seen, score, NEG)
            s_s[aligned(t, KTILE), :] = score
            return jnp.maximum(top, jnp.max(score.reshape(KTILE // 8, 8, rows), axis=0))

        top = lax.fori_loop(0, tiles, score_tile, jnp.full((8, rows), NEG, F32))
        top = jnp.max(top, axis=0, keepdims=True)
        acc_s[...] = jnp.zeros_like(acc_s)

        def prob_tile(t, total):
            at = pl.ds(pl.multiple_of(base + t * KTILE, BLK), KTILE)
            prob = jnp.exp2(s_s[aligned(t, KTILE), :] - top)
            rounded = prob.astype(BF16)
            p_s[aligned(t, KTILE), :] = rounded
            acc_s[...] += dot(vt_s[:, at], rounded, NN)
            return total + jnp.sum(prob.reshape(KTILE // 8, 8, rows), axis=0)

        total = lax.fori_loop(0, tiles, prob_tile, jnp.zeros((8, rows), F32))
        inverse = 1.0 / jnp.sum(total, axis=0, keepdims=True)
        att_t = (acc_s[...] * inverse).astype(BF16)
        g_t = dot(eye_d, gs, NT)
        q_t = dot(eye_d, qs, NT)
        delta = jnp.sum(g_t * att_t.astype(F32), axis=0, keepdims=True)
        g_n = (g_t * inverse).astype(BF16)
        q_n = (q_t * (inverse * SCALE)).astype(BF16)
        att = dot(eye_r, att_t, NT).astype(BF16)
        for h in range(heads):
            att_ref[here, h * HD:(h + 1) * HD] = att[h * BLK:(h + 1) * BLK]
        acc_s[...] = jnp.zeros_like(acc_s)

        def grad_tile(t, carry):
            at = pl.ds(pl.multiple_of(base + t * KTILE, BLK), KTILE)
            prob = p_s[aligned(t, KTILE), :]
            dprob = dot(v_s[at, :], gs, NT)
            dscore = (prob.astype(F32) * (dprob - delta)).astype(BF16)
            dv_s[at, :] += dot(prob, g_n, NT)
            dk_s[at, :] += dot(dscore, q_n, NT)
            acc_s[...] += dot(kt_s[:, at], dscore, NN)
            return carry

        lax.fori_loop(0, tiles, grad_tile, 0)
        dq_t = (acc_s[...] * (inverse * SCALE)).astype(BF16)
        dq = dot(eye_r, dq_t, NT).astype(BF16)
        for h in range(heads):
            dq_ref[here, h * HD:(h + 1) * HD] = dq[h * BLK:(h + 1) * BLK]
        return carry

    lax.fori_loop(0, own_blocks, query_block, 0)

    def hand_out(i, carry):
        src, dst = aligned(order_ref[i], BLK), aligned(i, BLK)
        dkv_ref[0, dst, :] = dk_s[src, :].astype(BF16)
        dkv_ref[1, dst, :] = dv_s[src, :].astype(BF16)
        return carry

    lax.fori_loop(0, blocks, hand_out, 0)


def attend(plane, q_loc, g_loc, kv, doc_ids, block_order):
    tokens = kv.shape[1]
    wide = q_loc.shape[1]
    rows = wide // HD * BLK
    padded = tokens + KTILE
    longest = (min(tokens, 4096) + BLK + KTILE - 1) // KTILE * KTILE
    vmem = pl.BlockSpec(memory_space=pltpu.VMEM)
    smem = pl.BlockSpec(memory_space=pltpu.SMEM)
    return pl.pallas_call(
        attend_kernel,
        out_shape=(
            jax.ShapeDtypeStruct(q_loc.shape, BF16),
            jax.ShapeDtypeStruct(q_loc.shape, BF16),
            jax.ShapeDtypeStruct(kv.shape, BF16),
        ),
        in_specs=[smem, smem, smem, vmem, vmem, vmem, pl.BlockSpec(memory_space=pl.ANY)],
        out_specs=(vmem, vmem, vmem),
        scratch_shapes=[
            pltpu.VMEM((padded, HD), BF16),
            pltpu.VMEM((padded, HD), BF16),
            pltpu.VMEM((HD, padded), BF16),
            pltpu.VMEM((HD, padded), BF16),
            pltpu.VMEM((padded, HD), F32),
            pltpu.VMEM((padded, HD), F32),
            pltpu.VMEM((longest, rows), F32),
            pltpu.VMEM((longest, rows), BF16),
            pltpu.VMEM((HD, rows), F32),
            pltpu.SemaphoreType.DMA((2,)),
        ],
        compiler_params=pltpu.CompilerParams(vmem_limit_bytes=VMEM_LIMIT),
        name="attend",
    )(block_order, doc_ids, plane, q_loc, g_loc, doc_ids.reshape(tokens // BLK, BLK), kv)


def scatter_kernel(planes, groups, att_ref, dq_ref, dkv_ref, ao_ref, dqo_ref, kg_ref, vg_ref,
                   mine_s, sib_s, stage_s, came_s, fin_s, land_s,
                   local, mine_sem, sib_send, sib_recv, a2a_send, a2a_recv, z_send, z_recv):
    at = Where(planes, groups)
    rows = ao_ref.shape[0]
    wide = att_ref.shape[1]
    half_rows = dkv_ref.shape[2] // 2
    hops = planes // 2
    mine = aligned(at.p, rows)
    cols = aligned(at.g * NS + at.s, wide)

    own_a = pltpu.make_async_copy(att_ref.at[mine], ao_ref.at[:, cols], local.at[0])
    own_q = pltpu.make_async_copy(dq_ref.at[mine], dqo_ref.at[:, cols], local.at[1])
    own_a.start()
    own_q.start()

    turns = [hops]
    for j in range(hops - 1, 0, -1):
        turns += [j, -j]
    turns += [0]
    own_part, sib_part = [], []
    for n, distance in enumerate(turns):
        chunk = (at.z + planes + distance) % planes
        own_part.append(pltpu.make_async_copy(dkv_ref.at[at.core, chunk], mine_s.at[chunk], mine_sem.at[n]))
        sib_part.append(remote(dkv_ref.at[1 - at.core, chunk], sib_s.at[chunk],
                               sib_send.at[n], sib_recv.at[n], at.sib))
    for copy in own_part:
        copy.start()
    at.greet()
    for copy in sib_part:
        copy.start()

    def send_out(i, carry):
        o, _, _, device = at.peer(i)
        theirs = aligned(o, rows)
        remote(att_ref.at[theirs], ao_ref.at[:, cols], a2a_send.at[0], a2a_recv.at[0], device).start()
        remote(dq_ref.at[theirs], dqo_ref.at[:, cols], a2a_send.at[1], a2a_recv.at[1], device).start()
        return carry

    lax.fori_loop(1, at.size, send_out, 0)

    def ready(distance):
        n = turns.index(distance)
        own_part[n].wait()
        sib_part[n].wait_recv()

    def own_sum(distance, half):
        chunk = (at.z + planes + distance) % planes
        part = pl.ds(half * half_rows, half_rows)
        return mine_s[chunk, part, :].astype(F32) + sib_s[chunk, part, :].astype(F32)

    def moves(j, half, way):
        return j > 0 or half == way

    def send(j, half, way):
        slot = (way, 2 * j + half)
        return remote(stage_s.at[slot], came_s.at[slot], z_send.at[slot], z_recv.at[slot],
                      at.up if way == 0 else at.down)

    for j in range(hops):
        distance = hops - j
        if j == 0:
            ready(hops)
        else:
            ready(distance)
            ready(-distance)
        for turn in (0, 1):
            for way in (0, 1):
                half = 1 - way if turn == 0 else way
                if not moves(j, half, way):
                    continue
                value = own_sum(distance if way == 0 else -distance, half)
                if j > 0 and moves(j - 1, half, way):
                    send(j - 1, half, way).wait_recv()
                    value = value + came_s[way, 2 * (j - 1) + half].astype(F32)
                stage_s[way, 2 * j + half] = value.astype(BF16)
                send(j, half, way).start()

    ready(0)
    for half in (0, 1):
        value = own_sum(0, half)
        for way in (0, 1):
            if moves(hops - 1, half, way):
                send(hops - 1, half, way).wait_recv()
                value = value + came_s[way, 2 * (hops - 1) + half].astype(F32)
        fin_s[pl.ds(half * half_rows, half_rows), :] = value.astype(BF16)

    group_cols = aligned(at.g, HD)
    target = land_s.at[at.core, at.ylo, :, group_cols]
    own_fin = pltpu.make_async_copy(fin_s.at[mine], target, local.at[2])
    own_fin.start()

    def send_fin(i, carry):
        o, _, _, device = at.peer(i)
        remote(fin_s.at[aligned(o, rows)], target, a2a_send.at[2], a2a_recv.at[2], device).start()
        return carry

    lax.fori_loop(1, at.size, send_fin, 0)

    others = pl.ds(0, rows * (at.size - 1))
    some = pl.ds(0, wide * (at.size - 1))
    own_a.wait()
    own_q.wait()
    for n, (src, dst) in enumerate(((att_ref, ao_ref), (dq_ref, dqo_ref))):
        sent, came = src.at[others], dst.at[:, some]
        remote(came, came, a2a_send.at[n], a2a_recv.at[n], at.up).wait_recv()
        remote(sent, sent, a2a_send.at[n], a2a_recv.at[n], at.up).wait_send()
    for j in range(hops):
        for half in (0, 1):
            for way in (0, 1):
                if moves(j, half, way):
                    send(j, half, way).wait_send()
    for copy in sib_part:
        copy.wait_send()
    own_fin.wait()
    moved = fin_s.at[others]
    remote(moved, moved, a2a_send.at[2], a2a_recv.at[2], at.up).wait()
    kg_ref[...] = (land_s[0, 0].astype(F32) + land_s[0, 1].astype(F32)).astype(BF16)
    vg_ref[...] = (land_s[1, 0].astype(F32) + land_s[1, 1].astype(F32)).astype(BF16)


def scatter(planes, groups, att, dq, dkv):
    plane_rows = att.shape[0]
    rows = plane_rows // (NS * groups)
    columns = att.shape[1] * NS * groups
    hops = planes // 2
    any_space = pl.BlockSpec(memory_space=pl.ANY)
    vmem = pl.BlockSpec(memory_space=pltpu.VMEM)
    dma = pltpu.SemaphoreType.DMA
    return pl.pallas_call(
        functools.partial(scatter_kernel, planes, groups),
        out_shape=(
            jax.ShapeDtypeStruct((rows, columns), BF16),
            jax.ShapeDtypeStruct((rows, columns), BF16),
            jax.ShapeDtypeStruct((rows, groups * HD), BF16),
            jax.ShapeDtypeStruct((rows, groups * HD), BF16),
        ),
        in_specs=[any_space] * 3,
        out_specs=(any_space, any_space, vmem, vmem),
        scratch_shapes=[
            pltpu.VMEM((planes, plane_rows, HD), BF16),
            pltpu.VMEM((planes, plane_rows, HD), BF16),
            pltpu.VMEM((2, 2 * hops, plane_rows // 2, HD), BF16),
            pltpu.VMEM((2, 2 * hops, plane_rows // 2, HD), BF16),
            pltpu.VMEM((plane_rows, HD), BF16),
            pltpu.VMEM((2, NS // 2, rows, groups * HD), BF16),
            dma((3,)),
            dma((planes,)),
            dma((planes,)),
            dma((planes,)),
            dma((3,)),
            dma((3,)),
            dma((2, 2 * hops)),
            dma((2, 2 * hops)),
        ],
        compiler_params=pltpu.CompilerParams(
            collective_id=1, has_side_effects=True, vmem_limit_bytes=VMEM_LIMIT
        ),
        name="scatter",
    )(att, dq, dkv)


def per_device(planes, groups, queries, keys, values, out_grad, doc_ids, block_order):
    plane = (lax.axis_index("ctx") // NS).astype(jnp.int32).reshape(1)
    q_loc, g_loc, kv = gather(planes, groups, queries, keys, values, out_grad)
    tokens = doc_ids.shape[0]
    att, dq, dkv = attend(plane, q_loc, g_loc, kv.reshape(2, tokens, HD), doc_ids, block_order)
    return scatter(planes, groups, att, dq, dkv.reshape(kv.shape))


def solution(mesh):
    split = P(("ctx", "head"), None)
    planes, groups = mesh.shape["ctx"] // NS, mesh.shape["head"]
    return jax.shard_map(
        functools.partial(per_device, planes, groups),
        mesh=mesh,
        in_specs=(split, split, split, split, P(), P()),
        out_specs=(split, split, split, split),
        check_vma=False,
    )
```

time: 699 us -> 137 us (0.20)
  local copies, waits for them, and re-layouts: 240 us -> 6.68 us
  starting transfers between devices: 180 us -> 0 us
  Pallas kernels: 0 us -> 130 us
  matrix products: 91.5 us -> 0 us
  other arithmetic: 83.5 us -> 0 us
  loops' own time: 50.1 us -> 0 us
  waiting for transfers between devices: 48.2 us -> 0 us
    gather x126 -> x0, local copies, waits for them, and re-layouts: 226 us -> none  [the longest x63 118 us: token_meta(): place = jnp.take(block_order, index // BLK) * BLK + index % BLK]
    ppermute x188 -> x0, starting transfers between devices: 148 us -> none  [passed_along(): lax.ppermute(shard, axis, [(i, (i + by) % devices) for i in range(devices)])]
    pallas_call x0 -> x3, Pallas kernels: none -> 130 us  [the longest x1 44.5 us: gather(): pl.pallas_call(functools.partial(gather_kernel, planes, groups), out_shap...]
    dot_general x168 -> x0, matrix products: 91.5 us -> none  [the longest x48 25.5 us: scores(): jnp.einsum('qgrd,kgd->grqk', q_grp, key_rows, preferred_element_type=jnp....]
    another operation x66 -> x0, loops' own time: 50.1 us -> none  [the longest x1 23.5 us: per_device(): lax.fori_loop(1, ranks, backward_step, (k_grp, v_grp, dk_acc, dv_acc, que...]
    reduce_or x62 -> x0, other arithmetic: 47.8 us -> none  [the longest x31 23.9 us: forward_tile(): jnp.any(visible)]
    all_to_all x8 -> x0, waiting for transfers between devices: 45 us -> none  [the longest x1 7.09 us: per_device(): lax.all_to_all(query_grad, 'head', split_axis=0, concat_axis=1, tiled=True)]
    all_to_all x8 -> x0, starting transfers between devices: 31.9 us -> none  [the longest x1 7.48 us: per_device(): lax.all_to_all(keys, 'head', split_axis=1, concat_axis=0, tiled=True)]
  transfers between devices with their start and end apart: 196 -> 0, of which waited for: 9 -> 0; matrix products, arithmetic and copies ran while one was open for 50% -> 0% of each run, Pallas kernels for 0% -> 0%
where the time goes in v1:
time: 137 us
  Pallas kernels  130 us (95%)
  local copies, waits for them, and re-layouts  6.68 us (5%)
    pallas_call x1, Pallas kernels, gather(): pl.pallas_call(functools.partial(gather_kernel, planes, groups), out_shap...  44.5 us
    pallas_call x1, Pallas kernels, scatter(): pl.pallas_call(functools.partial(scatter_kernel, planes, groups), out_sha...  43.5 us
    pallas_call x1, Pallas kernels, attend(): pl.pallas_call(attend_kernel, out_shape=(jax.ShapeDtypeStruct(q_loc.shape...  41.7 us
    unnamed x4, local copies, waits for them, and re-layouts  6.68 us

profile of v1, /device:TPU:1, one launch (start us, length us, event | category | flops | bytes accessed | tf_op | source)
XLA Modules:
  0.0 136.9 jit_solution(1583051927913252974)
XLA Ops:
  0.6 44.5 %gather.1 = (bf16[1024,256]{1,0:T(8,128)(2,1)}, bf16[1024,256]{1,0:T(8,128)(2,1)}, bf16[2,8,1024,128]{3,2,1,0:T(8,128)(2,1)}) custom-call(bf16[32,8192]{1,0:T(8,128)(2,1)} %q_ref.1, bf16[32,1024]{1,0:T(8,128)(2,1)} %k_ref.1, bf16[32,1024]{1,0:T(8,128)(2,1)} %v_ref.1, bf16[32,8192]{1,0:T(8,128)(2,1)} %g_ref.1), custom_call_target="tpu_custom_call" | custom-call | tf_op jit(solution)/shard_map/gather/pallas_call | solution.py:192
  45.1 41.7 %attend.1 = (bf16[1024,256]{1,0:T(8,128)(2,1)}, bf16[1024,256]{1,0:T(8,128)(2,1)}, bf16[2,8192,128]{2,1,0:T(8,128)(2,1)}) custom-call(s32[64]{0:T(128)} %order_ref.1, s32[8192]{0:T(1024)} %doc_ref.1, s32[1]{0:T(128)} %bitcast.plane_ref, bf16[1024,256]{1,0:T(8,128)(2,1)} %get-tuple-element.10.q_ref, bf16[1024,256]{1,0:T(8,128)(2,1)} %get-tuple-element.11.g_ref, ...), custom_call_target="tpu_custom_call" | custom-call | tf_op jit(solution)/shard_map/attend/pallas_call | solution.py:363
  86.8 43.5 %scatter.1 = (bf16[32,8192]{1,0:T(8,128)(2,1)}, bf16[32,8192]{1,0:T(8,128)(2,1)}, bf16[32,1024]{1,0:T(8,128)(2,1)}, bf16[32,1024]{1,0:T(8,128)(2,1)}) custom-call(bf16[1024,256]{1,0:T(8,128)(2,1)} %get-tuple-element.13.att_ref, bf16[1024,256]{1,0:T(8,128)(2,1)} %get-tuple-element.14.dq_ref, bf16[2,8,1024,128]{3,2,1,0:T(8,128)(2,1)} %bitcast.4), custom_call_target="tpu_custom_call" | custom-call | tf_op jit(solution)/shard_map/scatter/pallas_call | solution.py:518
  130.3 1.9 %copy.14 = bf16[32,8192]{1,0:T(8,128)(2,1)} copy(bf16[32,8192]{1,0:T(8,128)(2,1)} %get-tuple-element.20) | data formatting | bytes 1048576
  132.1 1.9 %copy.15 = bf16[32,8192]{1,0:T(8,128)(2,1)} copy(bf16[32,8192]{1,0:T(8,128)(2,1)} %get-tuple-element.21) | data formatting | bytes 1048576
  134.0 1.5 %copy.16 = bf16[32,1024]{1,0:T(8,128)(2,1)} copy(bf16[32,1024]{1,0:T(8,128)(2,1)} %get-tuple-element.22) | data formatting | bytes 131072
  135.5 1.5 %copy.17 = bf16[32,1024]{1,0:T(8,128)(2,1)} copy(bf16[32,1024]{1,0:T(8,128)(2,1)} %get-tuple-element.23) | data formatting | bytes 131072

commit v2 on v1

--- a/solution.py
+++ b/solution.py
@@ -13,7 +13,11 @@
 HD = 128
 BLK = 128
 NS = 4
-KTILE = 512
+KTILE = 2048
+PAIR = 2 * BLK
+LANES = 64
+OUT = 4
+FRONT = BLK
 LOG2E = math.log2(math.e)
 SCALE = 1.0 / math.sqrt(HD)
 NEG = -1e30
@@ -207,43 +211,44 @@
             pltpu.SemaphoreType.DMA,
             pltpu.SemaphoreType.DMA,
         ],
-        compiler_params=pltpu.CompilerParams(collective_id=0, has_side_effects=True),
+        compiler_params=pltpu.CompilerParams(
+            collective_id=0, has_side_effects=True, vmem_limit_bytes=VMEM_LIMIT
+        ),
         name="gather",
     )(queries, keys, values, out_grad)
 
 
-def attend_kernel(order_ref, doc_ref, plane_ref, q_ref, g_ref, doc2_ref, kv_ref, att_ref, dq_ref, dkv_ref,
-                  k_s, v_s, kt_s, vt_s, dk_s, dv_s, s_s, p_s, acc_s, sem):
+def attend_kernel(order_ref, doc_ref, plane_ref, doc2_ref, q_ref, g_ref, kv_ref, att_ref, dq_ref, dkv_ref,
+                  q_s, g_s, att_s, dq_s, kv_s, kvt_s, dkv_s, out_s, s_s, p_s, acc_s, top_s, total_s,
+                  begin_s, start_s, sem):
     tokens = kv_ref.shape[1]
     blocks = tokens // BLK
     own_blocks = q_ref.shape[0] // BLK
     heads = q_ref.shape[1] // HD
     rows = heads * BLK
-    padded = k_s.shape[0]
+    turned = min(tokens, 2048)
 
     def fetch(i, carry):
-        src, dst = aligned(i, BLK), aligned(order_ref[i], BLK)
-        pltpu.make_async_copy(kv_ref.at[0, src], k_s.at[dst], sem.at[0]).start()
-        pltpu.make_async_copy(kv_ref.at[1, src], v_s.at[dst], sem.at[1]).start()
+        dst = pl.ds(pl.multiple_of(FRONT + order_ref[i] * BLK, BLK), BLK)
+        pltpu.make_async_copy(kv_ref.at[:, aligned(i, BLK)], kv_s.at[:, dst], sem.at[0]).start()
         return carry
 
     lax.fori_loop(0, blocks, fetch, 0)
-    tail = pl.ds(tokens, padded - tokens)
-    k_s[tail, :] = jnp.zeros((padded - tokens, HD), BF16)
-    v_s[tail, :] = jnp.zeros((padded - tokens, HD), BF16)
-    kt_s[:, tail] = jnp.zeros((HD, padded - tokens), BF16)
-    vt_s[:, tail] = jnp.zeros((HD, padded - tokens), BF16)
+    load_q = pltpu.make_async_copy(q_ref, q_s, sem.at[2])
+    load_g = pltpu.make_async_copy(g_ref, g_s, sem.at[3])
+    load_q.start()
+    load_g.start()
+    head = pl.ds(0, FRONT)
+    kv_s[:, head, :] = jnp.zeros((2, FRONT, HD), BF16)
+    kvt_s[:, :, head] = jnp.zeros((2, HD, FRONT), BF16)
+    dkv_s[:, head, :] = jnp.zeros((2, FRONT, HD), F32)
 
     def clear(i, carry):
-        at = aligned(i, KTILE)
-        dk_s[at, :] = jnp.zeros((KTILE, HD), F32)
-        dv_s[at, :] = jnp.zeros((KTILE, HD), F32)
-        return carry
-
-    lax.fori_loop(0, padded // KTILE, clear, 0)
-    whole = pl.ds(0, tokens)
-    pltpu.make_async_copy(kv_ref.at[0], k_s.at[whole], sem.at[0]).wait()
-    pltpu.make_async_copy(kv_ref.at[1], v_s.at[whole], sem.at[1]).wait()
+        at = pl.ds(pl.multiple_of(FRONT + i * 512, BLK), 512)
+        dkv_s[:, at, :] = jnp.zeros((2, 512, HD), F32)
+        return carry
+
+    lax.fori_loop(0, tokens // 512, clear, 0)
 
     def eye(n):
         return (lax.broadcasted_iota(jnp.int32, (n, n), 0) == lax.broadcasted_iota(jnp.int32, (n, n), 1)).astype(
@@ -251,68 +256,118 @@
 
     eye_d = eye(HD)
     eye_r = eye(rows)
+    packed = [order_ref[plane_ref[0] * own_blocks + n] for n in range(own_blocks)]
+    firsts = [b * BLK for b in packed]
+    wanted = [doc_ref[first] for first in firsts]
+
+    def halve(_, spans):
+        lows, highs = [], []
+        for (lo, hi), doc0 in zip(spans, wanted):
+            mid = (lo + hi) // 2
+            below = doc_ref[mid] < doc0
+            lows.append(jnp.where(below, mid + 1, lo))
+            highs.append(jnp.where(below, hi, mid))
+        return tuple(zip(lows, highs))
+
+    spans = lax.fori_loop(0, tokens.bit_length(), halve, tuple((jnp.int32(0), first) for first in firsts))
+    starts = [lo for lo, _ in spans]
+    for n in range(own_blocks):
+        start_s[n] = starts[n]
+    lane = lax.broadcasted_iota(jnp.int32, (own_blocks, BLK), 1)
+    docs = jnp.concatenate([doc2_ref[pl.ds(b, 1), :] for b in packed], axis=0)
+    opens = (lane > 0) & (docs != pltpu.roll(docs, 1, 1))
+    first_of = jnp.concatenate([jnp.full((1, BLK), first, jnp.int32) for first in firsts], axis=0)
+    start_of = jnp.concatenate([jnp.full((1, BLK), start, jnp.int32) for start in starts], axis=0)
+    begin = jnp.where(opens, first_of + lane, start_of)
+    step = 1
+    while step < BLK:
+        begin = jnp.maximum(begin, jnp.where(lane >= step, pltpu.roll(begin, step, 1), 0))
+        step *= 2
+    begin_s[...] = begin
+    pltpu.make_async_copy(kv_ref, kv_s.at[:, pl.ds(FRONT, tokens)], sem.at[0]).wait()
 
     def turn(i, carry):
-        at = aligned(i, KTILE)
-        kt_s[:, at] = dot(eye_d, k_s[at, :], NT).astype(BF16)
-        vt_s[:, at] = dot(eye_d, v_s[at, :], NT).astype(BF16)
-        return carry
-
-    lax.fori_loop(0, tokens // KTILE, turn, 0)
+        at = pl.ds(pl.multiple_of(FRONT + i * turned, BLK), turned)
+        kvt_s[0, :, at] = dot(eye_d, kv_s[0, at, :], NT).astype(BF16)
+        kvt_s[1, :, at] = dot(eye_d, kv_s[1, at, :], NT).astype(BF16)
+        return carry
+
+    lax.fori_loop(0, tokens // turned, turn, 0)
 
     def query_block(n, carry):
         packed = order_ref[plane_ref[0] * own_blocks + n]
         first = packed * BLK
-        doc0 = doc_ref[first]
-
-        def halve(_, span):
-            lo, hi = span
-            mid = (lo + hi) // 2
-            below = doc_ref[mid] < doc0
-            return jnp.where(below, mid + 1, lo), jnp.where(below, hi, mid)
-
-        doc_start, _ = lax.fori_loop(0, tokens.bit_length(), halve, (jnp.int32(0), first))
-        base = (doc_start // BLK) * BLK
-        tiles = (first + BLK - base + KTILE - 1) // KTILE
-
-        lane = lax.broadcasted_iota(jnp.int32, (8, BLK), 1)
-        docs = jnp.broadcast_to(doc2_ref[pl.ds(packed, 1), :], (8, BLK))
-        opens = (lane > 0) & (docs != pltpu.roll(docs, 1, 1))
-        begin = jnp.where(opens, first + lane, doc_start)
-        step = 1
-        while step < BLK:
-            begin = jnp.maximum(begin, jnp.where(lane >= step, pltpu.roll(begin, step, 1), 0))
-            step *= 2
-        low = jnp.concatenate([begin[:1]] * heads, axis=1) - base
-        high = jnp.concatenate([(first + lane)[:1]] * heads, axis=1) - base
+        doc_start = start_s[n]
+        pairs = (first // BLK - doc_start // BLK + PAIR // BLK) // (PAIR // BLK)
+        base = FRONT + first + BLK - pairs * PAIR
+        lead = (pairs - 1) % (KTILE // PAIR) + 1
+        tiles = (pairs - 1) // (KTILE // PAIR)
+
+        def each_tile(work):
+            for size in range(1, KTILE // PAIR + 1):
+                @pl.when(lead == size)
+                def _():
+                    work(0, size * PAIR, True)
+
+            def step(t, carry):
+                work(pl.multiple_of(lead * PAIR + t * KTILE, PAIR), KTILE, False)
+                return carry
+
+            lax.fori_loop(0, tiles, step, 0)
+
+        begin = begin_s[pl.ds(n, 1), :]
+        lane = lax.broadcasted_iota(jnp.int32, (1, BLK), 1)
+        bias = jnp.where(begin > doc_start, NEG, 0.0)
+        bias = jnp.concatenate([bias] * heads, axis=1)
+        low = jnp.concatenate([begin] * heads, axis=1) + (FRONT - base)
+        high = jnp.concatenate([first + lane] * heads, axis=1) + (FRONT - base)
 
         here = aligned(n, BLK)
-        qs = jnp.concatenate([q_ref[here, h * HD:(h + 1) * HD] for h in range(heads)], axis=0)
-        gs = jnp.concatenate([g_ref[here, h * HD:(h + 1) * HD] for h in range(heads)], axis=0)
-        key_at = lax.broadcasted_iota(jnp.int32, (KTILE, rows), 0)
-
-        def score_tile(t, top):
-            at = pl.ds(pl.multiple_of(base + t * KTILE, BLK), KTILE)
-            score = dot(k_s[at, :], qs, NT) * (SCALE * LOG2E)
-            seen = (key_at >= low - t * KTILE) & (key_at <= high - t * KTILE)
-            score = jnp.where(seen, score, NEG)
-            s_s[aligned(t, KTILE), :] = score
-            return jnp.maximum(top, jnp.max(score.reshape(KTILE // 8, 8, rows), axis=0))
-
-        top = lax.fori_loop(0, tiles, score_tile, jnp.full((8, rows), NEG, F32))
-        top = jnp.max(top, axis=0, keepdims=True)
-        acc_s[...] = jnp.zeros_like(acc_s)
-
-        def prob_tile(t, total):
-            at = pl.ds(pl.multiple_of(base + t * KTILE, BLK), KTILE)
-            prob = jnp.exp2(s_s[aligned(t, KTILE), :] - top)
+        qs = jnp.concatenate([q_s[here, h * HD:(h + 1) * HD] for h in range(heads)], axis=0)
+        gs = jnp.concatenate([g_s[here, h * HD:(h + 1) * HD] for h in range(heads)], axis=0)
+
+        def score_tile(rel, width, leads):
+            score = dot(kv_s[0, pl.ds(pl.multiple_of(base + rel, BLK), width), :], qs, NT)
+            cuts = [(0, PAIR, True)] if leads else []
+            if leads and width > PAIR:
+                cuts += [(PAIR, width - BLK, False), (width - BLK, width, True)]
+            elif not leads:
+                cuts = [(0, width - BLK, False), (width - BLK, width, True)]
+            top = None
+            for start, end, edge in cuts:
+                count = end - start
+                part = score[start:end] * (SCALE * LOG2E)
+                if edge:
+                    key_at = lax.broadcasted_iota(jnp.int32, (count, rows), 0)
+                    seen = (key_at >= low - (rel + start)) & (key_at <= high - (rel + start))
+                    part = jnp.where(seen, part, NEG)
+                else:
+                    part = part + bias
+                s_s[pl.ds(pl.multiple_of(rel + start, BLK), count), :] = part
+                most = jnp.max(part.reshape(count // LANES, LANES, rows), axis=0)
+                top = most if top is None else jnp.maximum(top, most)
+            top_s[...] = top if leads else jnp.maximum(top_s[...], top)
+
+        each_tile(score_tile)
+        top = jnp.max(top_s[...], axis=0, keepdims=True)
+
+        def prob_tile(rel, width, leads):
+            at = pl.ds(pl.multiple_of(base + rel, BLK), width)
+            there = pl.ds(pl.multiple_of(rel, PAIR), width)
+            prob = jnp.exp2(s_s[there, :] - top)
             rounded = prob.astype(BF16)
-            p_s[aligned(t, KTILE), :] = rounded
-            acc_s[...] += dot(vt_s[:, at], rounded, NN)
-            return total + jnp.sum(prob.reshape(KTILE // 8, 8, rows), axis=0)
-
-        total = lax.fori_loop(0, tiles, prob_tile, jnp.zeros((8, rows), F32))
-        inverse = 1.0 / jnp.sum(total, axis=0, keepdims=True)
+            p_s[there, :] = rounded
+            part = dot(kvt_s[1, :, at], rounded, NN)
+            total = jnp.sum(prob.reshape(width // LANES, LANES, rows), axis=0)
+            if leads:
+                acc_s[...] = part
+                total_s[...] = total
+            else:
+                acc_s[...] += part
+                total_s[...] += total
+
+        each_tile(prob_tile)
+        inverse = 1.0 / jnp.sum(total_s[...], axis=0, keepdims=True)
         att_t = (acc_s[...] * inverse).astype(BF16)
         g_t = dot(eye_d, gs, NT)
         q_t = dot(eye_d, qs, NT)
@@ -321,45 +376,57 @@
         q_n = (q_t * (inverse * SCALE)).astype(BF16)
         att = dot(eye_r, att_t, NT).astype(BF16)
         for h in range(heads):
-            att_ref[here, h * HD:(h + 1) * HD] = att[h * BLK:(h + 1) * BLK]
-        acc_s[...] = jnp.zeros_like(acc_s)
-
-        def grad_tile(t, carry):
-            at = pl.ds(pl.multiple_of(base + t * KTILE, BLK), KTILE)
-            prob = p_s[aligned(t, KTILE), :]
-            dprob = dot(v_s[at, :], gs, NT)
+            att_s[here, h * HD:(h + 1) * HD] = att[h * BLK:(h + 1) * BLK]
+
+        def grad_tile(rel, width, leads):
+            at = pl.ds(pl.multiple_of(base + rel, BLK), width)
+            prob = p_s[pl.ds(pl.multiple_of(rel, PAIR), width), :]
+            dprob = dot(kv_s[1, at, :], gs, NT)
             dscore = (prob.astype(F32) * (dprob - delta)).astype(BF16)
-            dv_s[at, :] += dot(prob, g_n, NT)
-            dk_s[at, :] += dot(dscore, q_n, NT)
-            acc_s[...] += dot(kt_s[:, at], dscore, NN)
-            return carry
-
-        lax.fori_loop(0, tiles, grad_tile, 0)
+            dkv_s[1, at, :] += dot(prob, g_n, NT)
+            dkv_s[0, at, :] += dot(dscore, q_n, NT)
+            part = dot(kvt_s[0, :, at], dscore, NN)
+            if leads:
+                acc_s[...] = part
+            else:
+                acc_s[...] += part
+
+        each_tile(grad_tile)
         dq_t = (acc_s[...] * (inverse * SCALE)).astype(BF16)
         dq = dot(eye_r, dq_t, NT).astype(BF16)
         for h in range(heads):
-            dq_ref[here, h * HD:(h + 1) * HD] = dq[h * BLK:(h + 1) * BLK]
-        return carry
-
+            dq_s[here, h * HD:(h + 1) * HD] = dq[h * BLK:(h + 1) * BLK]
+        pltpu.make_async_copy(att_s.at[here], att_ref.at[here], sem.at[2]).start()
+        pltpu.make_async_copy(dq_s.at[here], dq_ref.at[here], sem.at[3]).start()
+        return carry
+
+    load_q.wait()
+    load_g.wait()
     lax.fori_loop(0, own_blocks, query_block, 0)
 
     def hand_out(i, carry):
-        src, dst = aligned(order_ref[i], BLK), aligned(i, BLK)
-        dkv_ref[0, dst, :] = dk_s[src, :].astype(BF16)
-        dkv_ref[1, dst, :] = dv_s[src, :].astype(BF16)
-        return carry
-
-    lax.fori_loop(0, blocks, hand_out, 0)
+        for j in range(OUT):
+            src = pl.ds(pl.multiple_of(FRONT + order_ref[i * OUT + j] * BLK, BLK), BLK)
+            dst = aligned(i * OUT + j, BLK)
+            out_s[:, dst, :] = dkv_s[:, src, :].astype(BF16)
+        dst = aligned(i, OUT * BLK)
+        pltpu.make_async_copy(out_s.at[:, dst], dkv_ref.at[:, dst], sem.at[1]).start()
+        return carry
+
+    lax.fori_loop(0, blocks // OUT, hand_out, 0)
+    pltpu.make_async_copy(att_s, att_ref, sem.at[2]).wait()
+    pltpu.make_async_copy(dq_s, dq_ref, sem.at[3]).wait()
+    pltpu.make_async_copy(out_s, dkv_ref, sem.at[1]).wait()
 
 
 def attend(plane, q_loc, g_loc, kv, doc_ids, block_order):
     tokens = kv.shape[1]
-    wide = q_loc.shape[1]
-    rows = wide // HD * BLK
-    padded = tokens + KTILE
-    longest = (min(tokens, 4096) + BLK + KTILE - 1) // KTILE * KTILE
+    rows = q_loc.shape[1] // HD * BLK
+    padded = FRONT + tokens
+    longest = (min(tokens, 4096) + BLK + PAIR - 1) // PAIR * PAIR
     vmem = pl.BlockSpec(memory_space=pltpu.VMEM)
     smem = pl.BlockSpec(memory_space=pltpu.SMEM)
+    any_space = pl.BlockSpec(memory_space=pl.ANY)
     return pl.pallas_call(
         attend_kernel,
         out_shape=(
@@ -367,27 +434,33 @@
             jax.ShapeDtypeStruct(q_loc.shape, BF16),
             jax.ShapeDtypeStruct(kv.shape, BF16),
         ),
-        in_specs=[smem, smem, smem, vmem, vmem, vmem, pl.BlockSpec(memory_space=pl.ANY)],
-        out_specs=(vmem, vmem, vmem),
+        in_specs=[smem, smem, smem, vmem, any_space, any_space, any_space],
+        out_specs=(any_space,) * 3,
         scratch_shapes=[
-            pltpu.VMEM((padded, HD), BF16),
-            pltpu.VMEM((padded, HD), BF16),
-            pltpu.VMEM((HD, padded), BF16),
-            pltpu.VMEM((HD, padded), BF16),
-            pltpu.VMEM((padded, HD), F32),
-            pltpu.VMEM((padded, HD), F32),
+            pltpu.VMEM(q_loc.shape, BF16),
+            pltpu.VMEM(q_loc.shape, BF16),
+            pltpu.VMEM(q_loc.shape, BF16),
+            pltpu.VMEM(q_loc.shape, BF16),
+            pltpu.VMEM((2, padded, HD), BF16),
+            pltpu.VMEM((2, HD, padded), BF16),
+            pltpu.VMEM((2, padded, HD), F32),
+            pltpu.VMEM((2, tokens, HD), BF16),
             pltpu.VMEM((longest, rows), F32),
             pltpu.VMEM((longest, rows), BF16),
             pltpu.VMEM((HD, rows), F32),
-            pltpu.SemaphoreType.DMA((2,)),
+            pltpu.VMEM((LANES, rows), F32),
+            pltpu.VMEM((LANES, rows), F32),
+            pltpu.VMEM((q_loc.shape[0] // BLK, BLK), jnp.int32),
+            pltpu.SMEM((q_loc.shape[0] // BLK,), jnp.int32),
+            pltpu.SemaphoreType.DMA((4,)),
         ],
         compiler_params=pltpu.CompilerParams(vmem_limit_bytes=VMEM_LIMIT),
         name="attend",
-    )(block_order, doc_ids, plane, q_loc, g_loc, doc_ids.reshape(tokens // BLK, BLK), kv)
-
-
-def scatter_kernel(planes, groups, att_ref, dq_ref, dkv_ref, ao_ref, dqo_ref, kg_ref, vg_ref,
-                   mine_s, sib_s, stage_s, came_s, fin_s, land_s,
+    )(block_order, doc_ids, plane, doc_ids.reshape(tokens // BLK, BLK), q_loc, g_loc, kv)
+
+
+def scatter_kernel(planes, groups, att_ref, dq_ref, dkv_ref, ao_ref, dqo_ref, land_s,
+                   mine_s, sib_s, stage_s, came_s, fin_s,
                    local, mine_sem, sib_send, sib_recv, a2a_send, a2a_recv, z_send, z_recv):
     at = Where(planes, groups)
     rows = ao_ref.shape[0]
@@ -503,8 +576,6 @@
     own_fin.wait()
     moved = fin_s.at[others]
     remote(moved, moved, a2a_send.at[2], a2a_recv.at[2], at.up).wait()
-    kg_ref[...] = (land_s[0, 0].astype(F32) + land_s[0, 1].astype(F32)).astype(BF16)
-    vg_ref[...] = (land_s[1, 0].astype(F32) + land_s[1, 1].astype(F32)).astype(BF16)
 
 
 def scatter(planes, groups, att, dq, dkv):
@@ -513,25 +584,22 @@
     columns = att.shape[1] * NS * groups
     hops = planes // 2
     any_space = pl.BlockSpec(memory_space=pl.ANY)
-    vmem = pl.BlockSpec(memory_space=pltpu.VMEM)
     dma = pltpu.SemaphoreType.DMA
     return pl.pallas_call(
         functools.partial(scatter_kernel, planes, groups),
         out_shape=(
             jax.ShapeDtypeStruct((rows, columns), BF16),
             jax.ShapeDtypeStruct((rows, columns), BF16),
-            jax.ShapeDtypeStruct((rows, groups * HD), BF16),
-            jax.ShapeDtypeStruct((rows, groups * HD), BF16),
+            jax.ShapeDtypeStruct((2, NS // 2, rows, groups * HD), BF16),
         ),
         in_specs=[any_space] * 3,
-        out_specs=(any_space, any_space, vmem, vmem),
+        out_specs=(any_space,) * 3,
         scratch_shapes=[
             pltpu.VMEM((planes, plane_rows, HD), BF16),
             pltpu.VMEM((planes, plane_rows, HD), BF16),
             pltpu.VMEM((2, 2 * hops, plane_rows // 2, HD), BF16),
             pltpu.VMEM((2, 2 * hops, plane_rows // 2, HD), BF16),
             pltpu.VMEM((plane_rows, HD), BF16),
-            pltpu.VMEM((2, NS // 2, rows, groups * HD), BF16),
             dma((3,)),
             dma((planes,)),
             dma((planes,)),
@@ -548,12 +616,39 @@
     )(att, dq, dkv)
 
 
+def finish_kernel(a_ref, q_ref, land_ref, ao_ref, qo_ref, kg_ref, vg_ref, sem):
+    moves = [pltpu.make_async_copy(a_ref, ao_ref, sem.at[0]), pltpu.make_async_copy(q_ref, qo_ref, sem.at[1])]
+    for move in moves:
+        move.start()
+    for part, out in ((0, kg_ref), (1, vg_ref)):
+        total = land_ref[part, 0].astype(F32)
+        for ylo in range(1, NS // 2):
+            total = total + land_ref[part, ylo].astype(F32)
+        out[...] = total.astype(BF16)
+    for move in moves:
+        move.wait()
+
+
+def finish(att, dq, land):
+    any_space = pl.BlockSpec(memory_space=pl.ANY)
+    vmem = pl.BlockSpec(memory_space=pltpu.VMEM)
+    grad = jax.ShapeDtypeStruct(land.shape[2:], BF16)
+    return pl.pallas_call(
+        finish_kernel,
+        out_shape=(jax.ShapeDtypeStruct(att.shape, BF16), jax.ShapeDtypeStruct(dq.shape, BF16), grad, grad),
+        in_specs=[any_space, any_space, vmem],
+        out_specs=(any_space, any_space, vmem, vmem),
+        scratch_shapes=[pltpu.SemaphoreType.DMA((2,))],
+        name="finish",
+    )(att, dq, land)
+
+
 def per_device(planes, groups, queries, keys, values, out_grad, doc_ids, block_order):
     plane = (lax.axis_index("ctx") // NS).astype(jnp.int32).reshape(1)
     q_loc, g_loc, kv = gather(planes, groups, queries, keys, values, out_grad)
     tokens = doc_ids.shape[0]
     att, dq, dkv = attend(plane, q_loc, g_loc, kv.reshape(2, tokens, HD), doc_ids, block_order)
-    return scatter(planes, groups, att, dq, dkv.reshape(kv.shape))
+    return finish(*scatter(planes, groups, att, dq, dkv.reshape(kv.shape)))
 
 
 def solution(mesh):

time: 137 us -> 143 us (1.044)
  Pallas kernels: 130 us -> 142 us
  local copies, waits for them, and re-layouts: 6.68 us -> 0 us
    pallas_call x0 -> x1, Pallas kernels: none -> 34.5 us  [finish(): pl.pallas_call(finish_kernel, out_shape=(jax.ShapeDtypeStruct(att.shape,...]
    pallas_call x1, Pallas kernels: 41.7 us -> 27.6 us  [attend(): pl.pallas_call(attend_kernel, out_shape=(jax.ShapeDtypeStruct(q_loc.shape...]
    pallas_call x1, Pallas kernels: 43.5 us -> 35.6 us  [scatter(): pl.pallas_call(functools.partial(scatter_kernel, planes, groups), out_sha...]
    unnamed x4 -> x0, local copies, waits for them, and re-layouts: 6.68 us -> none
where the time goes in v2:
time: 143 us
  Pallas kernels  142 us (99%)
    pallas_call x1, Pallas kernels, gather(): pl.pallas_call(functools.partial(gather_kernel, planes, groups), out_shap...  44.5 us
    pallas_call x1, Pallas kernels, scatter(): pl.pallas_call(functools.partial(scatter_kernel, planes, groups), out_sha...  35.6 us
    pallas_call x1, Pallas kernels, finish(): pl.pallas_call(finish_kernel, out_shape=(jax.ShapeDtypeStruct(att.shape,...  34.5 us
    pallas_call x1, Pallas kernels, attend(): pl.pallas_call(attend_kernel, out_shape=(jax.ShapeDtypeStruct(q_loc.shape...  27.6 us

profile of v2, /device:TPU:1, one launch (start us, length us, event | category | flops | bytes accessed | tf_op | source)
XLA Modules:
  0.0 142.8 jit_solution(11844418916328104850)
XLA Ops:
  0.6 44.5 %gather.1 = (bf16[1024,256]{1,0:T(8,128)(2,1)}, bf16[1024,256]{1,0:T(8,128)(2,1)}, bf16[2,8,1024,128]{3,2,1,0:T(8,128)(2,1)}) custom-call(bf16[32,8192]{1,0:T(8,128)(2,1)} %q_ref.1, bf16[32,1024]{1,0:T(8,128)(2,1)} %k_ref.1, bf16[32,1024]{1,0:T(8,128)(2,1)} %v_ref.1, bf16[32,8192]{1,0:T(8,128)(2,1)} %g_ref.1), custom_call_target="tpu_custom_call" | custom-call | tf_op jit(solution)/shard_map/gather/pallas_call | solution.py:196
  45.1 27.6 %attend.1 = (bf16[1024,256]{1,0:T(8,128)(2,1)}, bf16[1024,256]{1,0:T(8,128)(2,1)}, bf16[2,8192,128]{2,1,0:T(8,128)(2,1)}) custom-call(s32[64]{0:T(128)} %order_ref.1, s32[8192]{0:T(1024)} %doc_ref.1, s32[1]{0:T(128)} %bitcast.plane_ref, s32[64,128]{1,0:T(8,128)} %bitcast.6, bf16[1024,256]{1,0:T(8,128)(2,1)} %get-tuple-element.13.q_ref, ...), custom_call_target="tpu_custom_call" | custom-call | tf_op jit(solution)/shard_map/attend/pallas_call | solution.py:430
  72.7 35.6 %scatter.1 = (bf16[32,8192]{1,0:T(8,128)(2,1)}, bf16[32,8192]{1,0:T(8,128)(2,1)}, bf16[2,2,32,1024]{3,2,1,0:T(8,128)(2,1)}) custom-call(bf16[1024,256]{1,0:T(8,128)(2,1)} %get-tuple-element.16.att_ref, bf16[1024,256]{1,0:T(8,128)(2,1)} %get-tuple-element.17.dq_ref, bf16[2,8,1024,128]{3,2,1,0:T(8,128)(2,1)} %bitcast.4), custom_call_target="tpu_custom_call" | custom-call | tf_op jit(solution)/shard_map/scatter/pallas_call | solution.py:588
  108.3 34.5 %finish.1 = (bf16[32,8192]{1,0:T(8,128)(2,1)}, bf16[32,8192]{1,0:T(8,128)(2,1)}, bf16[32,1024]{1,0:T(8,128)(2,1)}, bf16[32,1024]{1,0:T(8,128)(2,1)}) custom-call(bf16[32,8192]{1,0:T(8,128)(2,1)} %get-tuple-element.19.a_ref, bf16[32,8192]{1,0:T(8,128)(2,1)} %get-tuple-element.20.q_ref, bf16[2,2,32,1024]{3,2,1,0:T(8,128)(2,1)} %get-tuple-element.21.land_ref), custom_call_target="tpu_custom_call" | custom-call | tf_op jit(solution)/shard_map/finish/pallas_call | solution.py:636

commit v3 on v2

--- a/solution.py
+++ b/solution.py
@@ -636,7 +636,7 @@
     return pl.pallas_call(
         finish_kernel,
         out_shape=(jax.ShapeDtypeStruct(att.shape, BF16), jax.ShapeDtypeStruct(dq.shape, BF16), grad, grad),
-        in_specs=[any_space, any_space, vmem],
+        in_specs=[vmem, vmem, vmem],
         out_specs=(any_space, any_space, vmem, vmem),
         scratch_shapes=[pltpu.SemaphoreType.DMA((2,))],
         name="finish",

time: 143 us -> 112 us (0.78)
  Pallas kernels: 142 us -> 111 us
    pallas_call x1, Pallas kernels: 34.5 us -> 2.9 us  [finish(): pl.pallas_call(finish_kernel, out_shape=(jax.ShapeDtypeStruct(att.shape,...]
    pallas_call x1, Pallas kernels: 35.6 us -> 38.8 us  [scatter(): pl.pallas_call(functools.partial(scatter_kernel, planes, groups), out_sha...]
    pallas_call x1, Pallas kernels: 27.6 us -> 24.6 us  [attend(): pl.pallas_call(attend_kernel, out_shape=(jax.ShapeDtypeStruct(q_loc.shape...]
where the time goes in v3:
time: 112 us; the launch traced here: 111 us
  Pallas kernels  111 us (99%)
    pallas_call x1, Pallas kernels, gather(): pl.pallas_call(functools.partial(gather_kernel, planes, groups), out_shap...  44.5 us
    pallas_call x1, Pallas kernels, scatter(): pl.pallas_call(functools.partial(scatter_kernel, planes, groups), out_sha...  38.8 us
    pallas_call x1, Pallas kernels, attend(): pl.pallas_call(attend_kernel, out_shape=(jax.ShapeDtypeStruct(q_loc.shape...  24.6 us
    pallas_call x1, Pallas kernels, finish(): pl.pallas_call(finish_kernel, out_shape=(jax.ShapeDtypeStruct(att.shape,...  2.9 us

profile of v3, /device:TPU:1, one launch (start us, length us, event | category | flops | bytes accessed | tf_op | source)
XLA Modules:
  0.0 111.4 jit_solution(8778217201267631998)
XLA Ops:
  0.6 44.5 %gather.1 = (bf16[1024,256]{1,0:T(8,128)(2,1)}, bf16[1024,256]{1,0:T(8,128)(2,1)}, bf16[2,8,1024,128]{3,2,1,0:T(8,128)(2,1)}) custom-call(bf16[32,8192]{1,0:T(8,128)(2,1)} %q_ref.1, bf16[32,1024]{1,0:T(8,128)(2,1)} %k_ref.1, bf16[32,1024]{1,0:T(8,128)(2,1)} %v_ref.1, bf16[32,8192]{1,0:T(8,128)(2,1)} %g_ref.1), custom_call_target="tpu_custom_call" | custom-call | tf_op jit(solution)/shard_map/gather/pallas_call | solution.py:196
  45.1 24.6 %attend.1 = (bf16[1024,256]{1,0:T(8,128)(2,1)}, bf16[1024,256]{1,0:T(8,128)(2,1)}, bf16[2,8192,128]{2,1,0:T(8,128)(2,1)}) custom-call(s32[64]{0:T(128)} %order_ref.1, s32[8192]{0:T(1024)} %doc_ref.1, s32[1]{0:T(128)} %bitcast.plane_ref, s32[64,128]{1,0:T(8,128)} %bitcast.6, bf16[1024,256]{1,0:T(8,128)(2,1)} %get-tuple-element.13.q_ref, ...), custom_call_target="tpu_custom_call" | custom-call | tf_op jit(solution)/shard_map/attend/pallas_call | solution.py:430
  69.7 38.8 %scatter.1 = (bf16[32,8192]{1,0:T(8,128)(2,1)}, bf16[32,8192]{1,0:T(8,128)(2,1)}, bf16[2,2,32,1024]{3,2,1,0:T(8,128)(2,1)}) custom-call(bf16[1024,256]{1,0:T(8,128)(2,1)} %get-tuple-element.16.att_ref, bf16[1024,256]{1,0:T(8,128)(2,1)} %get-tuple-element.17.dq_ref, bf16[2,8,1024,128]{3,2,1,0:T(8,128)(2,1)} %bitcast.4), custom_call_target="tpu_custom_call" | custom-call | tf_op jit(solution)/shard_map/scatter/pallas_call | solution.py:588
  108.5 2.9 %finish.1 = (bf16[32,8192]{1,0:T(8,128)(2,1)}, bf16[32,8192]{1,0:T(8,128)(2,1)}, bf16[32,1024]{1,0:T(8,128)(2,1)}, bf16[32,1024]{1,0:T(8,128)(2,1)}) custom-call(bf16[32,8192]{1,0:T(8,128)(2,1)} %get-tuple-element.19.a_ref, bf16[32,8192]{1,0:T(8,128)(2,1)} %get-tuple-element.20.q_ref, bf16[2,2,32,1024]{3,2,1,0:T(8,128)(2,1)} %get-tuple-element.21.land_ref), custom_call_target="tpu_custom_call" | custom-call | tf_op jit(solution)/shard_map/finish/pallas_call | solution.py:636

commit v4 on v3

--- a/solution.py
+++ b/solution.py
@@ -15,8 +15,14 @@
 NS = 4
 KTILE = 2048
 PAIR = 2 * BLK
-LANES = 64
-OUT = 4
+LANES = 32
+OUT = 8
+UNITS = 4
+ALONE = 1
+CARRIED = UNITS - ALONE
+OUT_AT = 0
+PIECES = 4
+FIRST_WAY = (0,)
 FRONT = BLK
 LOG2E = math.log2(math.e)
 SCALE = 1.0 / math.sqrt(HD)
@@ -45,19 +51,36 @@
         self.up = (((self.z + 1) % planes) * NS + self.s, self.g)
         self.down = (((self.z + planes - 1) % planes) * NS + self.s, self.g)
         self.sib = (ctx + 1 - 2 * self.core, self.g)
-
-    def peer(self, i):
-        o = (self.p + i) % self.size
-        return o, o // self.groups, o % self.groups, (self.z * NS + o // self.groups, o % self.groups)
+        self.other = (self.z * NS + lax.rem(self.s + 2, NS), self.g)
+
+        self.slots = [lax.rem(self.s + a, NS) for a in range(NS)]
+        self.ranks = [lax.rem(self.g + b, groups) for b in range(groups)]
+        self.lines = [self.z * NS + slot for slot in self.slots]
+
+    def unit(self, r):
+        return self.ylo * CARRIED + r if r < ALONE else r
+
+    def others_unit(self, r):
+        return (1 - self.ylo) * CARRIED + r
+
+    def peers(self, a):
+        return [(self.slots[a], rank, (self.lines[a], rank)) for b, rank in enumerate(self.ranks) if (a, b) != (0, 0)]
+
+    def each_peer(self, work):
+        for a in range(NS):
+
+            def step(b, carry):
+                rank = lax.rem(self.g + b, self.groups)
+                work(self.slots[a], rank, (self.lines[a], rank))
+                return carry
+
+            lax.fori_loop(0 if a else 1, self.groups, step, 0)
 
     def greet(self):
         bar = pltpu.get_barrier_semaphore()
-
-        def signal(i, carry):
-            pl.semaphore_signal(bar, inc=1, device_id=self.peer(i)[3], device_id_type=MESH)
-            return carry
-
-        lax.fori_loop(1, self.size, signal, 0)
+        for a in range(NS):
+            for _, _, device in self.peers(a):
+                pl.semaphore_signal(bar, inc=1, device_id=device, device_id_type=MESH)
         for other in (self.up, self.down):
             pl.semaphore_signal(bar, inc=1, device_id=other, device_id_type=MESH)
         pl.semaphore_wait(bar, self.size + 1)
@@ -74,11 +97,11 @@
 
 
 def gather_kernel(planes, groups, q_ref, k_ref, v_ref, g_ref, qo_ref, go_ref, kv_ref,
-                  local, a2a_send, a2a_recv, z_send, z_recv, sib_send, sib_recv):
+                  local, a2a_send, a2a_recv, z_send, z_recv, y_send, y_recv, sib_send, sib_recv):
     at = Where(planes, groups)
     rows = q_ref.shape[0]
     wide = q_ref.shape[1] // (NS * groups)
-    half_rows = kv_ref.shape[2] // 2
+    unit_rows = kv_ref.shape[2] // UNITS
     mine = aligned(at.p, rows)
     cols_own = aligned(at.g, HD)
 
@@ -99,74 +122,80 @@
 
     at.greet()
 
-    def send_kv(i, carry):
-        _, os, og, device = at.peer(i)
-        cols = aligned(og, HD)
-
-        @pl.when(os % 2 == 0)
-        def _():
-            remote(k_ref.at[:, cols], kv_ref.at[0, at.z, mine], a2a_send.at[0], a2a_recv.at[0], device).start()
-
-        @pl.when(os % 2 == 1)
-        def _():
-            remote(v_ref.at[:, cols], kv_ref.at[1, at.z, mine], a2a_send.at[0], a2a_recv.at[0], device).start()
-
-        return carry
-
-    lax.fori_loop(1, at.size, send_kv, 0)
-
-    def send_q(i, carry):
-        _, os, og, device = at.peer(i)
+    for a in range(NS):
+        for kind, source in ((0, k_ref), (1, v_ref)):
+            @pl.when(lax.rem(at.core + a, 2) == kind)
+            def _():
+                for _, og, device in at.peers(a):
+                    remote(source.at[:, aligned(og, HD)], kv_ref.at[kind, at.z, mine],
+                           a2a_send.at[0], a2a_recv.at[0], device).start()
+
+    def send_q(os, og, device):
         cols = aligned(og * NS + os, wide)
         remote(q_ref.at[:, cols], qo_ref.at[mine], a2a_send.at[1], a2a_recv.at[1], device).start()
         remote(g_ref.at[:, cols], go_ref.at[mine], a2a_send.at[2], a2a_recv.at[2], device).start()
-        return carry
-
-    lax.fori_loop(1, at.size, send_q, 0)
 
     others = pl.ds(0, rows * (at.size - 1))
     own_k.wait()
     got = kv_ref.at[at.core, at.z, others]
     remote(got, got, a2a_send.at[0], a2a_recv.at[0], at.up).wait_recv()
 
-    def piece(chunk, half):
-        return kv_ref.at[at.core, chunk, pl.ds(half * half_rows, half_rows)]
+    def piece(chunk, unit):
+        return kv_ref.at[at.core, chunk, pl.ds(pl.multiple_of(unit * unit_rows, unit_rows), unit_rows)]
 
     own = kv_ref.at[at.core, at.z]
     hops = planes // 2
 
-    def moves(j, half, way):
-        return j < hops - 1 or half == way
+    def moves(j, r, way):
+        return j < hops - 1 or (r in FIRST_WAY) == (way == 0)
 
     def chunk_at(j, way):
         return (at.z + planes - j) % planes if way == 0 else (at.z + j) % planes
 
-    def send(j, half, way):
-        ref = piece(chunk_at(j, way), half)
-        slot = (way, 2 * j + half)
+    def send(j, r, way):
+        ref = piece(chunk_at(j, way), at.unit(r))
+        slot = (way, CARRIED * j + r)
         return remote(ref, ref, z_send.at[slot], z_recv.at[slot], at.up if way == 0 else at.down)
 
-    def arrival(j, half, way):
-        ref = piece(chunk_at(j + 1, way), half)
-        slot = (way, 2 * j + half)
+    def arrival(j, r, way):
+        ref = piece(chunk_at(j + 1, way), at.unit(r))
+        slot = (way, CARRIED * j + r)
         return remote(ref, ref, z_send.at[slot], z_recv.at[slot], at.up if way == 0 else at.down)
 
-    for j in range(hops):
-        for half in (0, 1):
+    def across(j, r, way, unit):
+        ref = piece(chunk_at(j + 1, way), unit)
+        slot = (way, ALONE * j + r)
+        return remote(ref, ref, y_send.at[slot], y_recv.at[slot], at.other)
+
+    def to_sib(ref):
+        remote(ref, ref, sib_send, sib_recv, at.sib).start()
+
+    def take_across(j):
+        for r in range(ALONE):
+            for way in (0, 1):
+                if moves(j, r, way):
+                    across(j, r, way, at.others_unit(r)).wait_recv()
+                    to_sib(piece(chunk_at(j + 1, way), at.others_unit(r)))
+
+    for j in range(hops + 1):
+        for r in range(CARRIED):
             for way in (0, 1):
                 if j > 0:
-                    arrival(j - 1, half, way).wait_recv()
-                if moves(j, half, way):
-                    send(j, half, way).start()
+                    if not moves(j - 1, r, way):
+                        continue
+                    arrival(j - 1, r, way).wait_recv()
+                if j < hops and moves(j, r, way):
+                    send(j, r, way).start()
                 if j > 0:
-                    ref = piece(chunk_at(j, way), half)
-                    remote(ref, ref, sib_send, sib_recv, at.sib).start()
+                    if r < ALONE:
+                        across(j - 1, r, way, at.unit(r)).start()
+                    to_sib(piece(chunk_at(j, way), at.unit(r)))
         if j == 0:
-            remote(own, own, sib_send, sib_recv, at.sib).start()
-    for way in (0, 1):
-        arrival(hops - 1, way, way).wait_recv()
-        ref = piece(chunk_at(hops, way), way)
-        remote(ref, ref, sib_send, sib_recv, at.sib).start()
+            to_sib(own)
+            at.each_peer(send_q)
+        if j > 1:
+            take_across(j - 2)
+    take_across(hops - 1)
 
     own_q.wait()
     own_g.wait()
@@ -177,10 +206,12 @@
         remote(sent, sent, a2a_send.at[n + 1], a2a_recv.at[n + 1], at.up).wait_send()
     remote(got, got, a2a_send.at[0], a2a_recv.at[0], at.up).wait_send()
     for j in range(hops):
-        for half in (0, 1):
+        for r in range(CARRIED):
             for way in (0, 1):
-                if moves(j, half, way):
-                    send(j, half, way).wait_send()
+                if moves(j, r, way):
+                    send(j, r, way).wait_send()
+                    if r < ALONE:
+                        across(j, r, way, at.unit(r)).wait_send()
     sent = kv_ref.at[at.core]
     came = kv_ref.at[1 - at.core]
     remote(sent, sent, sib_send, sib_recv, at.sib).wait_send()
@@ -206,8 +237,10 @@
             pltpu.SemaphoreType.DMA((3,)),
             pltpu.SemaphoreType.DMA((3,)),
             pltpu.SemaphoreType.DMA((3,)),
-            pltpu.SemaphoreType.DMA((2, 2 * hops)),
-            pltpu.SemaphoreType.DMA((2, 2 * hops)),
+            pltpu.SemaphoreType.DMA((2, CARRIED * hops)),
+            pltpu.SemaphoreType.DMA((2, CARRIED * hops)),
+            pltpu.SemaphoreType.DMA((2, ALONE * hops)),
+            pltpu.SemaphoreType.DMA((2, ALONE * hops)),
             pltpu.SemaphoreType.DMA,
             pltpu.SemaphoreType.DMA,
         ],
@@ -226,7 +259,7 @@
     own_blocks = q_ref.shape[0] // BLK
     heads = q_ref.shape[1] // HD
     rows = heads * BLK
-    turned = min(tokens, 2048)
+    turned = min(tokens, 4096)
 
     def fetch(i, carry):
         dst = pl.ds(pl.multiple_of(FRONT + order_ref[i] * BLK, BLK), BLK)
@@ -465,7 +498,7 @@
     at = Where(planes, groups)
     rows = ao_ref.shape[0]
     wide = att_ref.shape[1]
-    half_rows = dkv_ref.shape[2] // 2
+    piece_rows = dkv_ref.shape[2] // PIECES
     hops = planes // 2
     mine = aligned(at.p, rows)
     cols = aligned(at.g * NS + at.s, wide)
@@ -491,14 +524,10 @@
     for copy in sib_part:
         copy.start()
 
-    def send_out(i, carry):
-        o, _, _, device = at.peer(i)
-        theirs = aligned(o, rows)
+    def send_out(os, og, device):
+        theirs = aligned(os * groups + og, rows)
         remote(att_ref.at[theirs], ao_ref.at[:, cols], a2a_send.at[0], a2a_recv.at[0], device).start()
         remote(dq_ref.at[theirs], dqo_ref.at[:, cols], a2a_send.at[1], a2a_recv.at[1], device).start()
-        return carry
-
-    lax.fori_loop(1, at.size, send_out, 0)
 
     def ready(distance):
         n = turns.index(distance)
@@ -507,14 +536,14 @@
 
     def own_sum(distance, half):
         chunk = (at.z + planes + distance) % planes
-        part = pl.ds(half * half_rows, half_rows)
+        part = pl.ds(half * piece_rows, piece_rows)
         return mine_s[chunk, part, :].astype(F32) + sib_s[chunk, part, :].astype(F32)
 
     def moves(j, half, way):
-        return j > 0 or half == way
+        return j > 0 or half * 2 // PIECES == way
 
     def send(j, half, way):
-        slot = (way, 2 * j + half)
+        slot = (way, PIECES * j + half)
         return remote(stage_s.at[slot], came_s.at[slot], z_send.at[slot], z_recv.at[slot],
                       at.up if way == 0 else at.down)
 
@@ -525,38 +554,37 @@
         else:
             ready(distance)
             ready(-distance)
-        for turn in (0, 1):
+        for turn in range(PIECES):
             for way in (0, 1):
-                half = 1 - way if turn == 0 else way
+                half = (turn + (1 - way) * PIECES // 2) % PIECES
                 if not moves(j, half, way):
                     continue
                 value = own_sum(distance if way == 0 else -distance, half)
                 if j > 0 and moves(j - 1, half, way):
                     send(j - 1, half, way).wait_recv()
-                    value = value + came_s[way, 2 * (j - 1) + half].astype(F32)
-                stage_s[way, 2 * j + half] = value.astype(BF16)
+                    value = value + came_s[way, PIECES * (j - 1) + half].astype(F32)
+                stage_s[way, PIECES * j + half] = value.astype(BF16)
                 send(j, half, way).start()
+        if j == OUT_AT:
+            at.each_peer(send_out)
 
     ready(0)
-    for half in (0, 1):
+    for half in range(PIECES):
         value = own_sum(0, half)
         for way in (0, 1):
             if moves(hops - 1, half, way):
                 send(hops - 1, half, way).wait_recv()
-                value = value + came_s[way, 2 * (hops - 1) + half].astype(F32)
-        fin_s[pl.ds(half * half_rows, half_rows), :] = value.astype(BF16)
+                value = value + came_s[way, PIECES * (hops - 1) + half].astype(F32)
+        fin_s[pl.ds(half * piece_rows, piece_rows), :] = value.astype(BF16)
 
     group_cols = aligned(at.g, HD)
     target = land_s.at[at.core, at.ylo, :, group_cols]
     own_fin = pltpu.make_async_copy(fin_s.at[mine], target, local.at[2])
     own_fin.start()
 
-    def send_fin(i, carry):
-        o, _, _, device = at.peer(i)
-        remote(fin_s.at[aligned(o, rows)], target, a2a_send.at[2], a2a_recv.at[2], device).start()
-        return carry
-
-    lax.fori_loop(1, at.size, send_fin, 0)
+    for a in range(NS):
+        for os, og, device in at.peers(a):
+            remote(fin_s.at[aligned(os * groups + og, rows)], target, a2a_send.at[2], a2a_recv.at[2], device).start()
 
     others = pl.ds(0, rows * (at.size - 1))
     some = pl.ds(0, wide * (at.size - 1))
@@ -567,7 +595,7 @@
         remote(came, came, a2a_send.at[n], a2a_recv.at[n], at.up).wait_recv()
         remote(sent, sent, a2a_send.at[n], a2a_recv.at[n], at.up).wait_send()
     for j in range(hops):
-        for half in (0, 1):
+        for half in range(PIECES):
             for way in (0, 1):
                 if moves(j, half, way):
                     send(j, half, way).wait_send()
@@ -597,8 +625,8 @@
         scratch_shapes=[
             pltpu.VMEM((planes, plane_rows, HD), BF16),
             pltpu.VMEM((planes, plane_rows, HD), BF16),
-            pltpu.VMEM((2, 2 * hops, plane_rows // 2, HD), BF16),
-            pltpu.VMEM((2, 2 * hops, plane_rows // 2, HD), BF16),
+            pltpu.VMEM((2, PIECES * hops, plane_rows // PIECES, HD), BF16),
+            pltpu.VMEM((2, PIECES * hops, plane_rows // PIECES, HD), BF16),
             pltpu.VMEM((plane_rows, HD), BF16),
             dma((3,)),
             dma((planes,)),
@@ -606,8 +634,8 @@
             dma((planes,)),
             dma((3,)),
             dma((3,)),
-            dma((2, 2 * hops)),
-            dma((2, 2 * hops)),
+            dma((2, PIECES * hops)),
+            dma((2, PIECES * hops)),
         ],
         compiler_params=pltpu.CompilerParams(
             collective_id=1, has_side_effects=True, vmem_limit_bytes=VMEM_LIMIT

time: 112 us -> 110 us (0.982); the launches traced: 111 us -> 108 us
  Pallas kernels: 111 us -> 107 us
    pallas_call x1, Pallas kernels: 38.8 us -> 33.6 us  [scatter(): pl.pallas_call(functools.partial(scatter_kernel, planes, groups), out_sha...]
    pallas_call x1, Pallas kernels: 24.6 us -> 27.2 us  [attend(): pl.pallas_call(attend_kernel, out_shape=(jax.ShapeDtypeStruct(q_loc.shape...]
where the time goes in v4:
time: 110 us; the launch traced here: 108 us
  Pallas kernels  107 us (97%)
    pallas_call x1, Pallas kernels, gather(): pl.pallas_call(functools.partial(gather_kernel, planes, groups), out_shap...  43.6 us
    pallas_call x1, Pallas kernels, scatter(): pl.pallas_call(functools.partial(scatter_kernel, planes, groups), out_sha...  33.6 us
    pallas_call x1, Pallas kernels, attend(): pl.pallas_call(attend_kernel, out_shape=(jax.ShapeDtypeStruct(q_loc.shape...  27.2 us
    pallas_call x1, Pallas kernels, finish(): pl.pallas_call(finish_kernel, out_shape=(jax.ShapeDtypeStruct(att.shape,...  2.9 us

profile of v4, /device:TPU:1, one launch (start us, length us, event | category | flops | bytes accessed | tf_op | source)
XLA Modules:
  0.0 108.0 jit_solution(10604241638365468523)
XLA Ops:
  0.6 43.6 %gather.1 = (bf16[1024,256]{1,0:T(8,128)(2,1)}, bf16[1024,256]{1,0:T(8,128)(2,1)}, bf16[2,8,1024,128]{3,2,1,0:T(8,128)(2,1)}) custom-call(bf16[32,8192]{1,0:T(8,128)(2,1)} %q_ref.1, bf16[32,1024]{1,0:T(8,128)(2,1)} %k_ref.1, bf16[32,1024]{1,0:T(8,128)(2,1)} %v_ref.1, bf16[32,8192]{1,0:T(8,128)(2,1)} %g_ref.1), custom_call_target="tpu_custom_call" | custom-call | tf_op jit(solution)/shard_map/gather/pallas_call | solution.py:227
  44.3 27.2 %attend.1 = (bf16[1024,256]{1,0:T(8,128)(2,1)}, bf16[1024,256]{1,0:T(8,128)(2,1)}, bf16[2,8192,128]{2,1,0:T(8,128)(2,1)}) custom-call(s32[64]{0:T(128)} %order_ref.1, s32[8192]{0:T(1024)} %doc_ref.1, s32[1]{0:T(128)} %bitcast.plane_ref, s32[64,128]{1,0:T(8,128)} %bitcast.6, bf16[1024,256]{1,0:T(8,128)(2,1)} %get-tuple-element.13.q_ref, ...), custom_call_target="tpu_custom_call" | custom-call | tf_op jit(solution)/shard_map/attend/pallas_call | solution.py:463
  71.5 33.6 %scatter.1 = (bf16[32,8192]{1,0:T(8,128)(2,1)}, bf16[32,8192]{1,0:T(8,128)(2,1)}, bf16[2,2,32,1024]{3,2,1,0:T(8,128)(2,1)}) custom-call(bf16[1024,256]{1,0:T(8,128)(2,1)} %get-tuple-element.16.att_ref, bf16[1024,256]{1,0:T(8,128)(2,1)} %get-tuple-element.17.dq_ref, bf16[2,8,1024,128]{3,2,1,0:T(8,128)(2,1)} %bitcast.4), custom_call_target="tpu_custom_call" | custom-call | tf_op jit(solution)/shard_map/scatter/pallas_call | solution.py:616
  105.1 2.9 %finish.1 = (bf16[32,8192]{1,0:T(8,128)(2,1)}, bf16[32,8192]{1,0:T(8,128)(2,1)}, bf16[32,1024]{1,0:T(8,128)(2,1)}, bf16[32,1024]{1,0:T(8,128)(2,1)}) custom-call(bf16[32,8192]{1,0:T(8,128)(2,1)} %get-tuple-element.19.a_ref, bf16[32,8192]{1,0:T(8,128)(2,1)} %get-tuple-element.20.q_ref, bf16[2,2,32,1024]{3,2,1,0:T(8,128)(2,1)} %get-tuple-element.21.land_ref), custom_call_target="tpu_custom_call" | custom-call | tf_op jit(solution)/shard_map/finish/pallas_call | solution.py:664
